TPU v7x, 32 devices: a whole 2x2x4 slice. The times are simulated.
32 devices in a mesh: ctx: 16 (over z, y, core), dp: 2 (over x).
Axes of the slice: x: 2, y: 2, z: 4, core: 2. Of those that a mesh axis runs over, the one named last changes fastest.
Arguments:
- features: bfloat16 [2, 3072, 1536], P('dp', 'ctx'), may hold values from -6 to 6
- bottleneck: bfloat16 [2, 3072, 384], P('dp', 'ctx'), may hold values from -6 to 6
- node_noise: bfloat16 [2, 3072, 1536], P('dp', 'ctx'), may hold values from -6 to 6
- targets: bfloat16 [2, 3072, 1536], P('dp', 'ctx'), may hold values from -15 to 15
- entry_weight: bfloat16 [384, 1536], P('ctx'), may hold values from -0.3125 to 0.3125
- conv_filters: bfloat16 [3, 1536, 384], P(None, None, 'ctx'), may hold values from -0.09375 to 0.09375
- exit_weight: bfloat16 [384, 1536], P('ctx'), may hold values from -0.3125 to 0.3125
Outputs:
- blended: bfloat16 [2, 3072, 1536], P('dp', 'ctx')
- estimate: float32 [384, 1536], P('ctx')
All inputs are finite; a program needn't handle non-finite values.
Results may differ from a plain program's by a relative error of at most 0.015.
The roundings to bfloat16 on the way count: a program that leaves them out, or rounds other values in their place, can miss the bound.
Values may be sent and summed in bfloat16 or wider, within the bound.
A program may use at most 64 MiB of HBM per device.

v0:
```python
import jax
import jax.numpy as jnp
from jax import lax
from jax.sharding import PartitionSpec as P

DILATION = 32


NOISE_SCALE = 0.1


def padded_2(cells, sides, width):
    for axis, dim in sides:
        count = lax.axis_size(axis)
        ends = count - 1
        head = lax.slice_in_dim(cells, 0, width, axis=dim)
        tail = lax.slice_in_dim(cells, cells.shape[dim] - width, cells.shape[dim], axis=dim)
        cells = jnp.concatenate(
            [
                lax.ppermute(tail, axis, [(i, (i + 1) % count) for i in range(ends)]),
                cells,
                lax.ppermute(head, axis, [((i + 1) % count, i) for i in range(ends)]),
            ],
            axis=dim,
        )
    return cells


def taps_for(padded, row_count, spacing, portion):
    summed = jnp.dot(padded[..., 0:row_count, :], portion[0], preferred_element_type=jnp.float32)
    summed = summed + jnp.dot(
        padded[..., spacing : spacing + row_count, :],
        portion[1],
        preferred_element_type=jnp.float32,
    )
    summed = summed + jnp.dot(
        padded[..., 2 * spacing : 2 * spacing + row_count, :],
        portion[2],
        preferred_element_type=jnp.float32,
    )
    return summed


def rows_for(left_side, portion):
    return jnp.dot(left_side, portion, preferred_element_type=jnp.float32)


def body(features, bottleneck, node_noise, targets, entry_weight, conv_filters, exit_weight):
    feats = features[0]
    bottle = bottleneck[0]
    jitter = node_noise[0]
    goal = targets[0].astype(jnp.float32)
    row_count = feats.shape[0]
    chan_count = feats.shape[1]
    spacing = DILATION
    baseline = feats.astype(jnp.float32) + rows_for(
        bottle, lax.all_gather(entry_weight, "ctx", axis=0, tiled=True)
    )
    offset_field = jitter.astype(jnp.float32) * NOISE_SCALE
    results = []
    for polarity in (1.0, -1.0):
        state = baseline + polarity * offset_field
        activated = jax.nn.gelu(state).astype(jnp.bfloat16)
        padded = padded_2(activated, (("ctx", 0),), spacing)
        mixed = taps_for(
            padded, row_count, spacing, lax.all_gather(conv_filters, "ctx", axis=2, tiled=True)
        )
        inner = jax.nn.gelu(mixed).astype(jnp.bfloat16)
        results.append(
            state + rows_for(inner, lax.all_gather(exit_weight, "ctx", axis=0, tiled=True))
        )
    upper = results[0]
    lower = results[1]
    blended = ((upper + lower) * 0.5).astype(jnp.bfloat16)[None]
    local_gap = jnp.sum((upper - lower) * (upper + lower - 2.0 * goal)) / (
        row_count * lax.axis_size("ctx") * chan_count
    )
    factor = lax.psum(local_gap, "ctx") / (2.0 * NOISE_SCALE)
    local_term = factor * lax.dot_general(
        bottle, jitter, (((0,), (0,)), ((), ())), preferred_element_type=jnp.float32
    )
    grouped = lax.psum(local_term, "dp")
    estimate = lax.psum_scatter(grouped, "ctx", scatter_dimension=0, tiled=True)
    return (blended, estimate)


def solution(mesh):
    return jax.shard_map(
        body,
        mesh=mesh,
        in_specs=(
            P("dp", "ctx", None),
            P("dp", "ctx", None),
            P("dp", "ctx", None),
            P("dp", "ctx", None),
            P("ctx", None),
            P(None, None, "ctx"),
            P("ctx", None),
        ),
        out_specs=(P("dp", "ctx", None), P("ctx", None)),
        check_vma=False,
    )
```

profile of v0, /device:TPU:0, one launch (start us, length us, event | category | flops | bytes accessed | tf_op | source)
XLA Modules:
  0.0 280.7 jit_solution(832804979618221188)
XLA Ops:
  7.2 0.0 copy-start
  7.2 0.0 all-gather.4.cloned.1.call-start
  7.2 0.7 all-gather.4.cloned.1.call-update
  7.9 0.0 all-gather.6.cloned.1.call-start
  8.0 0.7 all-gather.6.cloned.1.call-update
  8.7 0.0 all-gather.8.cloned.1.call-start
  8.7 0.7 all-gather.8.cloned.1.call-update
  9.4 0.0 reduce-scatter.2.cloned.1.call-start
  9.4 41.9 %all-gather.4.cloned.1.call-done = bf16[384,1536]{1,0:T(8,128)(2,1)} async-done(((bf16[24,1536]{1,0:T(8,128)(2,1)}), bf16[384,1536]{1,0:T(8,128)(2,1)}) %all-gather.4.cloned.1.call-update) | async-done | bytes 1179664 | tf_op jit(solution)/shard_map/all_gather | solution.py:57
  51.4 0.0 copy-done
  51.4 2.9 %fusion.17 = (bf16[192,1536]{1,0:T(8,128)(2,1)S(1)}, bf16[192,1536]{1,0:T(8,128)(2,1)S(1)}, f32[192,1536]{1,0:T(8,128)S(1)}) fusion(bf16[1,192,1536]{2,1,0:T(8,128)(2,1)} %param.9, bf16[384,1536]{1,0:T(8,128)(2,1)} %all-gather.4.cloned.1.call-done, bf16[1,192,384]{2,1,0:T(8,128)(2,1)S(1)} %copy-done, bf16[1,192,1536]{2,1,0:T(8,128)(2,1)} %param.7), kind=kOutput, calls=%fused_computation.25 | convolution fusion | flops 233865216 | bytes 4866048 | tf_op jit(solution)/shard_map/dot_general | solution.py:45
  54.2 0.0 copy-start.3
  54.3 1.3 collective-permute-start.3
  55.6 3.0 %collective-permute-start.2 = (bf16[32,1536]{1,0:T(8,128)(2,1)S(1)}, bf16[32,1536]{1,0:T(8,128)(2,1)S(1)}, u32[]{:S(2)}, u32[]{:S(2)}) collective-permute-start(bf16[32,1536]{1,0:T(8,128)(2,1)S(1)} %get-tuple-element.6), channel_id=1, source_target_pairs={{0,2},{2,4},{4,6},{6,8},{8,10},{10,12},{12,14},{14,16},{16,18},{18... | collective-permute-start | bytes 294920 | tf_op jit(solution)/shard_map/ppermute | solution.py:20
  58.6 1.3 collective-permute-start.1
  59.9 4.7 %collective-permute-start = (bf16[32,1536]{1,0:T(8,128)(2,1)S(1)}, bf16[32,1536]{1,0:T(8,128)(2,1)}, u32[]{:S(2)}, u32[]{:S(2)}) collective-permute-start(bf16[32,1536]{1,0:T(8,128)(2,1)S(1)} %get-tuple-element.8), channel_id=1, source_target_pairs={{0,2},{2,4},{4,6},{6,8},{8,10},{10,12},{12,14},{14,16},{16,18},{18... | collective-permute-start | bytes 294920 | tf_op jit(solution)/shard_map/ppermute | solution.py:20
  64.6 35.6 %all-gather.6.cloned.1.call-done = bf16[3,1536,384]{1,2,0:T(8,128)(2,1)} async-done(((bf16[3,1536,24]{1,2,0:T(8,128)(2,1)}), bf16[3,1536,384]{1,2,0:T(8,128)(2,1)}) %all-gather.6.cloned.1.call-update) | async-done | bytes 3538960 | tf_op jit(solution)/shard_map/all_gather | solution.py:66
  100.2 0.0 copy-done.3
  100.2 1.8 fusion.22
  102.0 0.0 copy-start.1
  102.1 0.0 collective-permute-done.3
  102.1 1.9 fusion.24
  104.0 35.9 %all-gather.8.cloned.1.call-done = bf16[384,1536]{1,0:T(8,128)(2,1)} async-done(((bf16[24,1536]{1,0:T(8,128)(2,1)}), bf16[384,1536]{1,0:T(8,128)(2,1)}) %all-gather.8.cloned.1.call-update) | async-done | bytes 1179664 | tf_op jit(solution)/shard_map/all_gather | solution.py:70
  139.9 0.0 collective-permute-done.2
  139.9 0.0 copy-done.1
  139.9 3.7 %convolution_add_fusion = f32[192,1536]{1,0:T(8,128)} fusion(bf16[384,1536]{1,0:T(8,128)(2,1)} %all-gather.8.cloned.1.call-done, f32[192,1536]{1,0:T(8,128)S(1)} %get-tuple-element.10, bf16[1,192,1536]{2,1,0:T(8,128)(2,1)S(1)} %copy-done.1, f32[192,384]{1,0:T(8,128)S(1)} %fusion.24, f32[192,384]{1,0:T(8,128)S(1)} %fusion.22, ...), kind=kOutput, calls=%fused_computation.1 | convolution fusion | flops 456155136 | bytes 6586368 | tf_op jit(solution)/shard_map/dot_general | solution.py:45
  143.6 0.0 copy-start.4
  143.6 2.8 fusion.23
  146.4 0.0 copy-start.2
  146.4 0.0 collective-permute-done.1
  146.4 0.0 copy-done.4
  146.4 0.0 copy-start.5
  146.4 2.7 fusion.25
  149.1 0.0 collective-permute-done
  149.1 0.0 copy-done.2
  149.1 0.0 copy-done.5
  149.1 4.7 %fusion.19 = (f32[]{:T(128)}, bf16[1,192,1536]{2,1,0:T(8,128)(2,1)}) fusion(bf16[1,192,1536]{2,1,0:T(8,128)(2,1)} %param.10, f32[192,1536]{1,0:T(8,128)} %convolution_add_fusion, bf16[384,1536]{1,0:T(8,128)(2,1)S(1)} %copy-done.2, f32[192,384]{1,0:T(8,128)} %fusion.25, f32[192,384]{1,0:T(8,128)S(1)} %copy-done.5, ...), kind=kOutput, calls=%fused_computation.31 | convolution fusion | flops 458809344 | bytes 7766020 | tf_op jit(solution)/shard_map/dot_general | solution.py:45
  154.5 32.2 %psum.14 = f32[]{:T(128)} all-reduce(f32[]{:T(128)S(6)} %div.6), channel_id=1, replica_groups=mesh['ctx'=16,'dp'=2] {'ctx'}, use_global_device_ids=true, to_apply=%region_1.0 | all-reduce | flops 1 | bytes 8 | tf_op jit(solution)/shard_map/psum | solution.py:78
  187.3 1.9 convolution_multiply_fusion
  189.2 0.0 reduce-scatter.2.cloned.1.call-update
  189.3 0.0 all-reduce.2.cloned.1.call-start
  189.3 60.3 %reduce-scatter.2.cloned.1.call-done = f32[24,1536]{1,0:T(8,128)} async-done(((f32[384,1536]{1,0:T(8,128)}), f32[24,1536]{1,0:T(8,128)}) %reduce-scatter.2.cloned.1.call-update) | async-done | bytes 147472 | tf_op jit(solution)/shard_map/reduce_scatter | solution.py:83
  249.6 0.0 all-reduce.2.cloned.1.call-update
  249.6 22.9 %all-reduce.2.cloned.1.call-done = f32[24,1536]{1,0:T(8,128)} async-done(((f32[24,1536]{1,0:T(8,128)}), f32[24,1536]{1,0:T(8,128)}) %all-reduce.2.cloned.1.call-update) | async-done | bytes 147472 | tf_op jit(solution)/shard_map/psum | solution.py:82
  272.6 1.6 copy.10
  (2 shorter events, 0.0 us)
Async XLA Ops:
  7.2 44.2 %copy-start = (bf16[1,192,384]{2,1,0:T(8,128)(2,1)S(1)}, bf16[1,192,384]{2,1,0:T(8,128)(2,1)}, u32[]{:S(2)}) copy-start(bf16[1,192,384]{2,1,0:T(8,128)(2,1)} %param.8) | copy-start | bytes 442372
  7.2 44.2 %all-gather.4.cloned.1.call-start = ((), (), s32[]{:S(2)}) async-start(), calls=%async_computation.1 | async-start | bytes 1253376 | tf_op jit(solution)/shard_map/all_gather | solution.py:57
  7.9 92.3 %all-gather.6.cloned.1.call-start = ((), (), s32[]{:S(2)}) async-start(), calls=%async_computation.2 | async-start | bytes 3760128 | tf_op jit(solution)/shard_map/all_gather | solution.py:66
  8.7 131.2 %all-gather.8.cloned.1.call-start = ((), (), s32[]{:S(2)}) async-start(), calls=%async_computation.3 | async-start | bytes 1253376 | tf_op jit(solution)/shard_map/all_gather | solution.py:70
  9.4 240.2 %reduce-scatter.2.cloned.1.call-start = ((), (), s32[]{:S(2)}) async-start(), calls=%async_computation.4 | async-start | bytes 2506752 | tf_op jit(solution)/shard_map/reduce_scatter | solution.py:83
  54.2 46.0 %copy-start.3 = (bf16[192,1536]{1,0:T(8,128)(2,1)}, bf16[192,1536]{1,0:T(8,128)(2,1)S(1)}, u32[]{:S(2)}) copy-start(bf16[192,1536]{1,0:T(8,128)(2,1)S(1)} %get-tuple-element.5) | copy-start | bytes 1769476
  54.3 47.8 %collective-permute-start.3 = (bf16[32,1536]{1,0:T(8,128)(2,1)S(1)}, bf16[32,1536]{1,0:T(8,128)(2,1)}, u32[]{:S(2)}, u32[]{:S(2)}) collective-permute-start(bf16[32,1536]{1,0:T(8,128)(2,1)S(1)} %get-tuple-element.7), channel_id=1, source_target_pairs={{2,0},{4,2},{6,4},{8,6},{10,8},{12,10},{14,12},{16,14},{18,16},{20... | collective-permute-start | bytes 294920 | tf_op jit(solution)/shard_map/ppermute | solution.py:22
  55.6 84.3 %collective-permute-start.2 = (bf16[32,1536]{1,0:T(8,128)(2,1)S(1)}, bf16[32,1536]{1,0:T(8,128)(2,1)S(1)}, u32[]{:S(2)}, u32[]{:S(2)}) collective-permute-start(bf16[32,1536]{1,0:T(8,128)(2,1)S(1)} %get-tuple-element.6), channel_id=1, source_target_pairs={{0,2},{2,4},{4,6},{6,8},{8,10},{10,12},{12,14},{14,16},{16,18},{18... | collective-permute-start | bytes 294920 | tf_op jit(solution)/shard_map/ppermute | solution.py:20
  58.6 87.8 %collective-permute-start.1 = (bf16[32,1536]{1,0:T(8,128)(2,1)S(1)}, bf16[32,1536]{1,0:T(8,128)(2,1)}, u32[]{:S(2)}, u32[]{:S(2)}) collective-permute-start(bf16[32,1536]{1,0:T(8,128)(2,1)S(1)} %get-tuple-element.9), channel_id=1, source_target_pairs={{2,0},{4,2},{6,4},{8,6},{10,8},{12,10},{14,12},{16,14},{18,16},{20... | collective-permute-start | bytes 294920 | tf_op jit(solution)/shard_map/ppermute | solution.py:22
  59.9 89.2 %collective-permute-start = (bf16[32,1536]{1,0:T(8,128)(2,1)S(1)}, bf16[32,1536]{1,0:T(8,128)(2,1)}, u32[]{:S(2)}, u32[]{:S(2)}) collective-permute-start(bf16[32,1536]{1,0:T(8,128)(2,1)S(1)} %get-tuple-element.8), channel_id=1, source_target_pairs={{0,2},{2,4},{4,6},{6,8},{8,10},{10,12},{12,14},{14,16},{16,18},{18... | collective-permute-start | bytes 294920 | tf_op jit(solution)/shard_map/ppermute | solution.py:20
  102.0 37.8 %copy-start.1 = (bf16[1,192,1536]{2,1,0:T(8,128)(2,1)S(1)}, bf16[1,192,1536]{2,1,0:T(8,128)(2,1)}, u32[]{:S(2)}) copy-start(bf16[1,192,1536]{2,1,0:T(8,128)(2,1)} %param.9) | copy-start | bytes 1769476
  143.6 2.8 copy-start.4
  146.4 2.7 copy-start.2
  146.4 2.7 copy-start.5
  189.3 83.3 %all-reduce.2.cloned.1.call-start = ((), (), s32[]{:S(2)}) async-start(), calls=%async_computation.5 | async-start | bytes 294912 | tf_op jit(solution)/shard_map/psum | solution.py:82
Sparse Core Ops, SparseCore 0:
  10.3 41.0 all-gather.3
  53.6 46.5 all-gather.5
  102.5 37.3 all-gather.7
  189.4 60.1 reduce-scatter.1
  251.8 20.7 all-reduce.1
where the time goes:
time: 281 us
  waiting for transfers between devices  199 us (71%)
  blocking collectives  32.2 us (11%)
  matrix products  22.5 us (8%)
  between operations  15.2 us (5%)
  starting transfers between devices  10.5 us (4%)
    reduce_scatter x1, waiting for transfers between devices, body(): estimate = lax.psum_scatter(grouped, 'ctx', scatter_dimension=0, tiled=True)  60.3 us
    all_gather x1, waiting for transfers between devices, body(): lax.all_gather(entry_weight, 'ctx', axis=0, tiled=True)  41.9 us
    all_gather x1, waiting for transfers between devices, body(): lax.all_gather(exit_weight, 'ctx', axis=0, tiled=True)  35.9 us
    all_gather x1, waiting for transfers between devices, body(): lax.all_gather(conv_filters, 'ctx', axis=2, tiled=True)  35.6 us
    psum x1, blocking collectives, body(): factor = lax.psum(local_gap, 'ctx') / (2.0 * NOISE_SCALE)  32.2 us
    psum x1, waiting for transfers between devices, body(): grouped = lax.psum(local_term, 'dp')  22.9 us
    dot_general x3, matrix products, rows_for(): return jnp.dot(left_side, portion, preferred_element_type=jnp.float32)  11.3 us
    ppermute x2, starting transfers between devices, padded_2(): lax.ppermute(tail, axis, [(i, (i + 1) % count) for i in range(ends)])  7.69 us
  transfers between devices with their start and end apart: 9, of which 5 were waited for; matrix products, arithmetic and copies ran while one was open for 6% of the time, Pallas kernels for 0%

commit v1 on v0

--- a/solution.py
+++ b/solution.py
@@ -1,6 +1,10 @@
+import functools
+
 import jax
 import jax.numpy as jnp
 from jax import lax
+from jax.experimental import pallas as pl
+from jax.experimental.pallas import tpu as pltpu
 from jax.sharding import PartitionSpec as P
 
 DILATION = 32
@@ -84,9 +88,414 @@
     return (blended, estimate)
 
 
+F32 = jnp.float32
+BF16 = jnp.bfloat16
+GROUP = 256
+PHASES = ((0, 1), (1, 3), (4, 1))
+HOPS = ((4, 3), (3, 4))
+
+
+def chip_at(position, chips):
+    return jnp.where(position < chips // 2, 2 * position, 2 * (chips - 1 - position) + 1)
+
+
+def kernel(
+    chips,
+    feats, bottle, noise, goal, wpad,
+    blended, estimate,
+    weights, wpeer, fx, nx, bx, act, base, inner,
+    keep, csend, crecv, ysend, yrecv, zsend, zrecv, xsend, xrecv, pair, prow, gaps1, gaps2,
+    ring_recv, x_recv, core_recv, bulk_send, init_send, init_recv, halo_send, halo_recv, rs_send, rs_recv,
+):
+    rows, chans = feats.shape
+    bot = bottle.shape[1]
+    unit = wpad.shape[2]
+    half = chans // 2
+    groups = chans // GROUP
+    side = groups // 2
+    zs = chips // 2
+    others = chips - 1
+    dp = lax.axis_index("dp")
+    ctx = lax.axis_index("ctx")
+    count = 2 * chips
+    core = lax.rem(ctx, 2)
+    chip = ctx // 2
+    yy = lax.rem(chip, 2)
+    zz = chip // 2
+    par = lax.rem(dp, 2)
+    mate = dp + 1 - 2 * par
+    place = jnp.where(yy == 0, zz, chips - 1 - zz)
+
+    def at(d, z, y, c):
+        return {"dp": d, "ctx": (z * 2 + y) * 2 + c}
+
+    def on_ring(p):
+        return lax.rem(p + chips, chips)
+
+    twin = at(dp, zz, yy, 1 - core)
+    across = at(mate, zz, yy, core)
+    near = [(i, j, k) for i in range(2) for j in range(2) for k in range(2) if i or j or k]
+
+    def near_dev(i, j, k):
+        return at(
+            mate if i else dp,
+            zz,
+            1 - yy if j else yy,
+            1 - core if k else core,
+        )
+
+    left = {"dp": dp, "ctx": lax.rem(ctx + count - 1, count)}
+    right = {"dp": dp, "ctx": lax.rem(ctx + 1, count)}
+    line = [at(dp, lax.rem(zz + d, zs), yy, core) for d in range(1, zs)]
+    peers = [near_dev(*n) for n in near] + line + [left, right]
+
+    barrier = pltpu.get_barrier_semaphore()
+    for peer in peers:
+        pl.semaphore_signal(barrier, inc=1, device_id=peer, device_id_type=pl.DeviceIdType.MESH)
+    pl.semaphore_wait(barrier, len(peers))
+
+    def remote(src, dst, ssem, rsem, dev):
+        c = pltpu.make_async_remote_copy(
+            src_ref=src, dst_ref=dst, send_sem=ssem, recv_sem=rsem,
+            device_id=dev, device_id_type=pl.DeviceIdType.MESH,
+        )
+        return c
+
+    def drain(ref, sem):
+        pltpu.make_async_copy(ref, ref, sem).wait()
+
+    mine = pl.ds(core * side, side)
+    theirs = pl.ds((1 - core) * side, side)
+    inits = []
+    for n, (first, size) in enumerate(PHASES):
+        inits.append(
+            remote(
+                wpad.at[theirs, pl.ds(first, size)], wpeer.at[theirs, pl.ds(first, size)],
+                init_send.at[n], init_recv.at[n], twin,
+            )
+        )
+    inits.append(remote(wpad.at[mine], wpeer.at[mine], init_send.at[3], init_recv.at[3], twin))
+    for c in inits:
+        c.start()
+    halos = []
+    for n, (src, dst) in enumerate(((feats, fx), (noise, nx), (bottle, bx))):
+        w = DILATION
+        halos.append(
+            remote(src.at[pl.ds(0, w)], dst.at[pl.ds(w + rows, w)], halo_send.at[2 * n], halo_recv.at[2 * n], left)
+        )
+        halos.append(
+            remote(src.at[pl.ds(rows - w, w)], dst.at[pl.ds(0, w)], halo_send.at[2 * n + 1], halo_recv.at[2 * n + 1], right)
+        )
+    for c in halos:
+        c.start()
+
+    own_rows = pl.ds(pl.multiple_of(chip * unit, 16), unit)
+    g_ring = (core * side, core * side + 1 + par)
+    g_x = core * side + 2 - par
+
+    def piece(n, g, q):
+        first, size = PHASES[n]
+        return weights.at[g, pl.ds(first, size), pl.ds(pl.multiple_of(q * unit, 16), unit), :]
+
+    def slot(n, j, d, h):
+        return n * 2 * others + j * others + (h - 1 if d == 0 else HOPS[j][0] + h - 1)
+
+    def origin(d, h):
+        return chip_at(on_ring(place - h if d == 0 else place + h), chips)
+
+    def toward(d):
+        q = chip_at(on_ring(place + 1 if d == 0 else place - 1), chips)
+        return {"dp": dp, "ctx": q * 2 + core}
+
+    nexts = (toward(0), toward(1))
+
+    def ring_copy(n, j, d, h):
+        q = origin(d, h - 1)
+        p = piece(n, g_ring[j], q)
+        return remote(p, p, bulk_send.at[0], ring_recv.at[slot(n, j, d, h)], nexts[d])
+
+    def ring_wait(n, j, d, h):
+        p = piece(n, g_ring[j], origin(d, h))
+        remote(p, p, bulk_send.at[0], ring_recv.at[slot(n, j, d, h)], nexts[d]).wait_recv()
+
+    def to_twin(n, g, q):
+        p = piece(n, g, q)
+        remote(p, p, bulk_send.at[2], core_recv.at[n], twin).start()
+
+    def hop(n, h):
+        for j in range(2):
+            for d in range(2):
+                if h > HOPS[j][d]:
+                    continue
+                ring_wait(n, j, d, h)
+                if h < HOPS[j][d]:
+                    ring_copy(n, j, d, h + 1).start()
+                q = origin(d, h)
+                if j == 1:
+                    p = piece(n, g_ring[1], q)
+                    remote(p, p, bulk_send.at[1], x_recv.at[n * others + slot(0, 1, d, h) - others], across).start()
+        for j in range(2):
+            for d in range(2):
+                if h <= HOPS[j][d]:
+                    to_twin(n, g_ring[j], origin(d, h))
+
+    def xhop(n, h):
+        for d in range(2):
+            if h > HOPS[1][d]:
+                continue
+            q = origin(d, h)
+            p = piece(n, g_x, q)
+            remote(p, p, bulk_send.at[1], x_recv.at[n * others + slot(0, 1, d, h) - others], across).wait_recv()
+            to_twin(n, g_x, q)
+
+    def settle(n):
+        first, size = PHASES[n]
+        drain(weights.at[pl.ds(0, side), pl.ds(first, size), pl.ds(0, others * unit)], core_recv.at[n])
+
+    def assemble(n, begin):
+        first, size = PHASES[n]
+        for g in range(side):
+            for m in range(first, first + size):
+                weights[begin + g, m, own_rows, :] = wpad[begin + g, m] + wpeer[begin + g, m]
+
+    def launch(n):
+        p = remote(wpad.at[mine, pl.ds(*PHASES[n])], wpeer.at[mine, pl.ds(*PHASES[n])], init_send.at[n], init_recv.at[n], twin)
+        p.wait_recv()
+        assemble(n, core * side)
+        for j in range(2):
+            for d in range(2):
+                ring_copy(n, j, d, 1).start()
+
+    launch(0)
+    launch(1)
+    w = DILATION
+    fx[w:w + rows, :] = feats[...]
+    nx[w:w + rows, :] = noise[...]
+    bx[w:w + rows, :] = bottle[...]
+    hop(0, 1)
+
+    def outer(g):
+        cols = pl.ds(pl.multiple_of(g * GROUP, GROUP), GROUP)
+        return lax.dot_general(bottle[...], noise[:, cols], (((0,), (0,)), ((), ())), preferred_element_type=F32)
+
+    for g in range(side):
+        csend[:, :, g * GROUP:(g + 1) * GROUP] = outer((1 - core) * side + g).astype(BF16).reshape(chips, unit, GROUP)
+    rs_core = remote(csend, crecv, rs_send.at[0], rs_recv.at[0], twin)
+    rs_core.start()
+    hop(0, 2)
+    launch(2)
+    for g in range(side):
+        keep[:, :, g * GROUP:(g + 1) * GROUP] = outer(core * side + g).reshape(chips, unit, GROUP)
+    hop(0, 3)
+    xhop(0, 1)
+    rs_core.wait_recv()
+    for z in range(zs):
+        ysend[z] = (keep[2 * z + 1 - yy] + crecv[2 * z + 1 - yy].astype(F32)).astype(BF16)
+    rs_y = remote(ysend, yrecv, rs_send.at[1], rs_recv.at[1], near_dev(0, 1, 0))
+    rs_y.start()
+    hop(0, 4)
+    xhop(0, 2)
+    hop(1, 1)
+    xhop(0, 3)
+    xhop(0, 4)
+    remote(wpad.at[theirs], wpeer.at[theirs], init_send.at[3], init_recv.at[3], twin).wait_recv()
+    for n in range(3):
+        assemble(n, (1 - core) * side)
+    for c in halos:
+        c.wait()
+    rs_y.wait_recv()
+    for z in range(zs):
+        total = keep[2 * z + yy] + crecv[2 * z + yy].astype(F32) + yrecv[z].astype(F32)
+        keep[2 * z + yy] = total
+        zsend[z] = total.astype(BF16)
+    rs_z = []
+    for d in range(1, zs):
+        c = remote(zsend.at[lax.rem(zz + d, zs)], zrecv.at[d - 1], rs_send.at[1 + d], rs_recv.at[1 + d], line[d - 1])
+        c.start()
+        rs_z.append(c)
+    settle(0)
+
+    edge = lax.broadcasted_iota(jnp.int32, (rows + 2 * w, 1), 0)
+    inside = jnp.logical_and(
+        jnp.logical_or(edge >= w, ctx > 0), jnp.logical_or(edge < w + rows, ctx < count - 1)
+    )
+
+    def enter(g):
+        cols = pl.ds(g * GROUP, GROUP)
+        b = fx[:, cols].astype(F32) + jnp.dot(bx[...], weights[g, 0], preferred_element_type=F32)
+        off = nx[:, cols].astype(F32) * NOISE_SCALE
+        base[:, cols] = b[w:w + rows]
+        for p, state in enumerate((b + off, b - off)):
+            act[p, :, cols] = jnp.where(inside, jax.nn.gelu(state), 0.0).astype(BF16)
+
+    enter(0)
+    enter(1)
+    hop(1, 2)
+    xhop(1, 1)
+    enter(2)
+    enter(3)
+    hop(1, 3)
+    xhop(1, 2)
+    enter(4)
+    enter(5)
+    hop(1, 4)
+    xhop(1, 3)
+    hop(2, 1)
+    xhop(1, 4)
+    hop(2, 2)
+    xhop(2, 1)
+    for c in rs_z:
+        c.wait_recv()
+    owned = keep[chip]
+    for d in range(zs - 1):
+        owned = owned + zrecv[d].astype(F32)
+    pair[par] = owned
+    xsend[...] = owned.astype(BF16)
+    rs_x = remote(xsend, xrecv, rs_send.at[1 + zs], rs_recv.at[1 + zs], across)
+    rs_x.start()
+    settle(1)
+
+    def mix(k, p):
+        total = jnp.zeros((rows, bot), F32)
+        for g in range(groups):
+            total = total + lax.dot_general(
+                act[p, k * w:k * w + rows, g * GROUP:(g + 1) * GROUP], weights[g, 1 + k],
+                (((1,), (1,)), ((), ())), preferred_element_type=F32,
+            )
+        return total
+
+    def mixed(p):
+        inner[p] = jax.nn.gelu(mix(0, p) + mix(1, p) + mix(2, p)).astype(BF16)
+
+    mixed(0)
+    hop(2, 3)
+    xhop(2, 2)
+    mixed(1)
+    hop(2, 4)
+    xhop(2, 3)
+    xhop(2, 4)
+    rs_x.wait_recv()
+    pair[1 - par] = xrecv[...].astype(F32)
+    give = pl.ds(pl.multiple_of((1 - core) * (unit // 2), 8), unit // 2)
+    have = pl.ds(pl.multiple_of(core * (unit // 2), 8), unit // 2)
+    rs_f = remote(pair.at[:, give, :], prow, rs_send.at[2 + zs], rs_recv.at[2 + zs], twin)
+    rs_f.start()
+    settle(2)
+
+    lanes = jnp.zeros((1, GROUP), F32)
+    for g in range(groups):
+        cols = pl.ds(g * GROUP, GROUP)
+        off = noise[:, cols].astype(F32) * NOISE_SCALE
+        b = base[:, cols]
+        upper = b + off + jnp.dot(inner[0], weights[g, 4], preferred_element_type=F32)
+        lower = b - off + jnp.dot(inner[1], weights[g, 4], preferred_element_type=F32)
+        both = upper + lower
+        blended[:, cols] = (both * 0.5).astype(BF16)
+        lanes = lanes + jnp.sum((upper - lower) * (both - 2.0 * goal[:, cols].astype(F32)), axis=0, keepdims=True)
+    local = jnp.sum(lanes, axis=1, keepdims=True) / (rows * count * chans)
+    shelf = lax.broadcasted_iota(jnp.int32, (8, 128), 0)
+    gaps1[0] = jnp.where(shelf == par, local, 0.0)
+    sent = []
+    for i, n in enumerate(near):
+        c = remote(gaps1.at[0], gaps1.at[i + 1], bulk_send.at[3], bulk_send.at[4], near_dev(*n))
+        c.start()
+    drain(gaps1.at[pl.ds(1, len(near))], bulk_send.at[4])
+    drain(gaps1.at[pl.ds(1, len(near))], bulk_send.at[3])
+    gaps2[0] = jnp.sum(gaps1[...], axis=0)
+    for d in range(1, zs):
+        remote(gaps2.at[0], gaps2.at[d], bulk_send.at[5], bulk_send.at[6], line[d - 1]).start()
+    rs_f.wait()
+    drain(gaps2.at[pl.ds(1, zs - 1)], bulk_send.at[6])
+    drain(gaps2.at[pl.ds(1, zs - 1)], bulk_send.at[5])
+    factors = jnp.sum(gaps2[...], axis=0) / (2.0 * NOISE_SCALE)
+    f0 = factors[0:1, 0:1]
+    f1 = factors[1:2, 0:1]
+    here = pl.ds(pl.multiple_of(core * half, 128), half)
+    there = pl.ds(pl.multiple_of((1 - core) * half, 128), half)
+    estimate[:, here] = f0 * pair[0, have, :] + f1 * pair[1, have, :]
+    estimate[:, there] = f0 * prow[0] + f1 * prow[1]
+
+    rs_core.wait_send()
+    rs_y.wait_send()
+    rs_x.wait_send()
+    for c in rs_z:
+        c.wait_send()
+    for c in inits:
+        c.wait_send()
+    for n, ways in enumerate((2, 1, 3)):
+        drain(weights.at[pl.ds(0, ways), :, pl.ds(0, others * unit)], bulk_send.at[n])
+
+
+def fused(features, bottleneck, node_noise, targets, entry_weight, conv_filters, exit_weight):
+    count = lax.axis_size("ctx")
+    chips = count // 2
+    _, rows, chans = features.shape
+    bot = bottleneck.shape[2]
+    share = entry_weight.shape[0]
+    unit = 2 * share
+    groups = chans // GROUP
+    zs = chips // 2
+    core = lax.axis_index("ctx") % 2
+    shard = jnp.concatenate([entry_weight[None], jnp.swapaxes(conv_filters, 1, 2), exit_weight[None]], axis=0)
+    shard = shard.reshape(5, share, groups, GROUP).transpose(2, 0, 1, 3)
+    none = jnp.zeros_like(shard)
+    wpad = jnp.concatenate(
+        [jnp.where(core == 0, shard, none), jnp.where(core == 1, shard, none)], axis=2
+    )
+    wide = rows + 2 * DILATION
+    half = chans // 2
+    blended, estimate = pl.pallas_call(
+        functools.partial(kernel, chips),
+        out_shape=(
+            jax.ShapeDtypeStruct((rows, chans), BF16),
+            jax.ShapeDtypeStruct((share, chans), F32),
+        ),
+        in_specs=[pl.BlockSpec(memory_space=pltpu.VMEM)] * 5,
+        out_specs=[pl.BlockSpec(memory_space=pltpu.VMEM)] * 2,
+        scratch_shapes=[
+            pltpu.VMEM((groups, 5, bot, GROUP), BF16),
+            pltpu.VMEM((groups, 5, unit, GROUP), BF16),
+            pltpu.VMEM((wide, chans), BF16),
+            pltpu.VMEM((wide, chans), BF16),
+            pltpu.VMEM((wide, bot), BF16),
+            pltpu.VMEM((2, wide, chans), BF16),
+            pltpu.VMEM((rows, chans), F32),
+            pltpu.VMEM((2, rows, bot), BF16),
+            pltpu.VMEM((chips, unit, half), F32),
+            pltpu.VMEM((chips, unit, half), BF16),
+            pltpu.VMEM((chips, unit, half), BF16),
+            pltpu.VMEM((zs, unit, half), BF16),
+            pltpu.VMEM((zs, unit, half), BF16),
+            pltpu.VMEM((zs, unit, half), BF16),
+            pltpu.VMEM((zs - 1, unit, half), BF16),
+            pltpu.VMEM((unit, half), BF16),
+            pltpu.VMEM((unit, half), BF16),
+            pltpu.VMEM((2, unit, half), F32),
+            pltpu.VMEM((2, unit // 2, half), F32),
+            pltpu.VMEM((8, 8, 128), F32),
+            pltpu.VMEM((zs, 8, 128), F32),
+            pltpu.SemaphoreType.DMA((3 * 2 * (chips - 1),)),
+            pltpu.SemaphoreType.DMA((3 * (chips - 1),)),
+            pltpu.SemaphoreType.DMA((3,)),
+            pltpu.SemaphoreType.DMA((7,)),
+            pltpu.SemaphoreType.DMA((4,)),
+            pltpu.SemaphoreType.DMA((4,)),
+            pltpu.SemaphoreType.DMA((6,)),
+            pltpu.SemaphoreType.DMA((6,)),
+            pltpu.SemaphoreType.DMA((3 + zs,)),
+            pltpu.SemaphoreType.DMA((3 + zs,)),
+        ],
+        compiler_params=pltpu.CompilerParams(
+            collective_id=0, has_side_effects=True, vmem_limit_bytes=48 * 1024 * 1024
+        ),
+    )(features[0], bottleneck[0], node_noise[0], targets[0], wpad)
+    return blended[None], estimate
+
+
 def solution(mesh):
+    small = mesh.shape["ctx"] == 16 and mesh.shape["dp"] == 2
     return jax.shard_map(
-        body,
+        fused if small else body,
         mesh=mesh,
         in_specs=(
             P("dp", "ctx", None),

time: 281 us -> 71.1 us (0.25)
  waiting for transfers between devices: 199 us -> 0 us
  Pallas kernels: 0 us -> 64.3 us
  blocking collectives: 32.2 us -> 0 us
  matrix products: 22.5 us -> 0 us
  between operations: 15.2 us -> 0.73 us
  starting transfers between devices: 10.5 us -> 0 us
  local copies, waits for them, and re-layouts: 1.64 us -> 5.75 us
    all_gather x3 -> x0, waiting for transfers between devices: 113 us -> none  [the longest x1 41.9 us: body(): lax.all_gather(entry_weight, 'ctx', axis=0, tiled=True)]
    pallas_call x0 -> x1, Pallas kernels: none -> 64.3 us  [fused(): pl.pallas_call(functools.partial(kernel, chips), out_shape=(jax.ShapeDtyp...]
    reduce_scatter x1 -> x0, waiting for transfers between devices: 60.3 us -> none  [body(): estimate = lax.psum_scatter(grouped, 'ctx', scatter_dimension=0, tiled=True)]
    psum x1 -> x0, blocking collectives: 32.2 us -> none  [body(): factor = lax.psum(local_gap, 'ctx') / (2.0 * NOISE_SCALE)]
    psum x1 -> x0, waiting for transfers between devices: 22.9 us -> none  [body(): grouped = lax.psum(local_term, 'dp')]
    dot_general x8 -> x0, matrix products: 22.5 us -> none  [the longest x3 11.3 us: rows_for(): return jnp.dot(left_side, portion, preferred_element_type=jnp.float32)]
    ppermute x4 -> x0, starting transfers between devices: 10.3 us -> none  [the longest x2 7.69 us: padded_2(): lax.ppermute(tail, axis, [(i, (i + 1) % count) for i in range(ends)])]
  transfers between devices with their start and end apart: 9 -> 0, of which waited for: 5 -> 0; matrix products, arithmetic and copies ran while one was open for 6% -> 0% of each run, Pallas kernels for 0% -> 0%
where the time goes in v1:
time: 71.1 us; the launch traced here: 70.8 us
  Pallas kernels  64.3 us (90%)
  local copies, waits for them, and re-layouts  5.75 us (8%)
  between operations  0.73 us (1%)
    pallas_call x1, Pallas kernels, fused(): pl.pallas_call(functools.partial(kernel, chips), out_shape=(jax.ShapeDtyp...  64.3 us
    unnamed x12, local copies, waits for them, and re-layouts  3.76 us
    concatenate x3, local copies, waits for them, and re-layouts, fused(): jnp.concatenate([entry_weight[None], jnp.swapaxes(conv_filters, 1, 2), ex...  1.99 us

profile of v1, /device:TPU:0, one launch (start us, length us, event | category | flops | bytes accessed | tf_op | source)
XLA Modules:
  0.0 70.8 jit_solution(12114707422711204891)
XLA Ops:
  0.6 1.0 %concatenate.13 = bf16[1,24,6,256]{3,2,1,0:T(8,128)(2,1)S(1)} reshape(bf16[24,1536]{1,0:T(8,128)(2,1)} %param.11) | data formatting | bytes 147456 | tf_op jit(solution)/shard_map/concatenate | solution.py:439
  1.6 1.0 %concatenate.15 = bf16[1,24,6,256]{3,2,1,0:T(8,128)(2,1)S(1)} reshape(bf16[24,1536]{1,0:T(8,128)(2,1)} %param.13) | data formatting | bytes 147456 | tf_op jit(solution)/shard_map/concatenate | solution.py:439
  2.6 1.0 %bitcast_dynamic-update-slice_fusion = bf16[5,24,6,256]{3,1,0,2:T(8,128)(2,1)S(1)} fusion(bf16[5,24,6,256]{3,1,0,2:T(8,128)(2,1)S(1)} %copy_dynamic-update-slice_fusion.1, bf16[3,3,6,8,256]{4,3,2,1,0:T(8,128)(2,1)} %bitcast.18), kind=kLoop, calls=%fused_computation.3 | loop fusion | bytes 442368
  3.6 0.0 copy-start.2
  3.6 0.1 select_bitcast_fusion.1
  3.7 0.0 copy-start
  3.7 0.0 copy-start.1
  3.7 0.0 copy-start.3
  3.7 0.1 pad_maximum_fusion.wpad
  3.8 0.9 %copy-done.2 = bf16[1,192,1536]{2,1,0:T(8,128)(2,1)S(1)} copy-done((bf16[1,192,1536]{2,1,0:T(8,128)(2,1)S(1)}, bf16[1,192,1536]{2,1,0:T(8,128)(2,1)}, u32[]{:S(2)}) %copy-start.2) | copy-done | bytes 589848
  4.7 0.2 copy-done
  4.9 0.2 copy-done.1
  5.1 0.0 copy-done.3
  5.1 64.3 %shard_map.86 = (bf16[192,1536]{1,0:T(8,128)(2,1)S(1)}, f32[24,1536]{1,0:T(8,128)S(1)}) custom-call(bf16[192,1536]{1,0:T(8,128)(2,1)S(1)} %bitcast.14, bf16[192,384]{1,0:T(8,128)(2,1)S(1)} %bitcast.17, bf16[192,1536]{1,0:T(8,128)(2,1)S(1)} %bitcast.15, bf16[192,1536]{1,0:T(8,128)(2,1)S(1)} %bitcast.16, bf16[6,5,48,256]{3,2,1,0:T(8,128)(2,1)S(1)} %pad_maximum_fusion.wpad), custom_call_target="tpu_custom_call" | custom-call | tf_op jit(solution)/shard_map/pallas_call | solution.py:447
  69.4 0.8 %copy.20 = bf16[1,192,1536]{2,1,0:T(8,128)(2,1)} copy(bf16[1,192,1536]{2,1,0:T(8,128)(2,1)S(1)} %bitcast.13) | data formatting | bytes 1179648
  70.2 0.7 copy.21
  (2 shorter events, 0.0 us)
Async XLA Ops:
  3.6 1.1 %copy-start.2 = (bf16[1,192,1536]{2,1,0:T(8,128)(2,1)S(1)}, bf16[1,192,1536]{2,1,0:T(8,128)(2,1)}, u32[]{:S(2)}) copy-start(bf16[1,192,1536]{2,1,0:T(8,128)(2,1)} %param.10) | copy-start | bytes 1769476
  3.7 1.2 %copy-start = (bf16[1,192,1536]{2,1,0:T(8,128)(2,1)S(1)}, bf16[1,192,1536]{2,1,0:T(8,128)(2,1)}, u32[]{:S(2)}) copy-start(bf16[1,192,1536]{2,1,0:T(8,128)(2,1)} %param.7) | copy-start | bytes 1769476
  3.7 1.4 %copy-start.1 = (bf16[1,192,1536]{2,1,0:T(8,128)(2,1)S(1)}, bf16[1,192,1536]{2,1,0:T(8,128)(2,1)}, u32[]{:S(2)}) copy-start(bf16[1,192,1536]{2,1,0:T(8,128)(2,1)} %param.9) | copy-start | bytes 1769476
  3.7 1.4 %copy-start.3 = (bf16[1,192,384]{2,1,0:T(8,128)(2,1)S(1)}, bf16[1,192,384]{2,1,0:T(8,128)(2,1)}, u32[]{:S(2)}) copy-start(bf16[1,192,384]{2,1,0:T(8,128)(2,1)} %param.8) | copy-start | bytes 442372

commit v2 on v1

--- a/solution.py
+++ b/solution.py
@@ -92,7 +92,7 @@
 BF16 = jnp.bfloat16
 GROUP = 256
 PHASES = ((0, 1), (1, 3), (4, 1))
-HOPS = ((4, 3), (3, 4))
+HOPS = 4
 
 
 def chip_at(position, chips):
@@ -101,15 +101,16 @@
 
 def kernel(
     chips,
-    feats, bottle, noise, goal, wpad,
+    feats, bottle, noise, goal, entry, filters, leave,
     blended, estimate,
-    weights, wpeer, fx, nx, bx, act, base, inner,
+    weights, wpad, wpeer, fx, nx, bx, gx, act, base, mixed, inner,
     keep, csend, crecv, ysend, yrecv, zsend, zrecv, xsend, xrecv, pair, prow, gaps1, gaps2,
-    ring_recv, x_recv, core_recv, bulk_send, init_send, init_recv, halo_send, halo_recv, rs_send, rs_recv,
+    ring_recv, x_recv, core_recv, bulk_send, init_send, init_recv, halo_send, halo_recv, rs_send, rs_recv, load,
 ):
     rows, chans = feats.shape
     bot = bottle.shape[1]
-    unit = wpad.shape[2]
+    share = entry.shape[0]
+    unit = 2 * share
     half = chans // 2
     groups = chans // GROUP
     side = groups // 2
@@ -149,6 +150,27 @@
     line = [at(dp, lax.rem(zz + d, zs), yy, core) for d in range(1, zs)]
     peers = [near_dev(*n) for n in near] + line + [left, right]
 
+    w = DILATION
+    middle = pl.ds(w, rows)
+    loads = [
+        pltpu.make_async_copy(src, dst, load.at[n])
+        for n, (src, dst) in enumerate(
+            (
+                (bottle, bx.at[middle]), (noise, nx.at[middle]), (feats, fx.at[middle]), (goal, gx),
+            )
+        )
+    ]
+    for c in loads:
+        c.start()
+    blank = jnp.zeros((share, GROUP), F32)
+    for g in range(groups):
+        for m in range(5):
+            shard = entry if m == 0 else leave if m == 4 else filters.at[m - 1]
+            part = shard[:, g * GROUP:(g + 1) * GROUP].astype(F32)
+            low = jnp.concatenate([part, blank], axis=0)
+            high = jnp.concatenate([blank, part], axis=0)
+            wpad[g, m] = jnp.where(core == 0, low, high).astype(BF16)
+
     barrier = pltpu.get_barrier_semaphore()
     for peer in peers:
         pl.semaphore_signal(barrier, inc=1, device_id=peer, device_id_type=pl.DeviceIdType.MESH)
@@ -179,7 +201,6 @@
         c.start()
     halos = []
     for n, (src, dst) in enumerate(((feats, fx), (noise, nx), (bottle, bx))):
-        w = DILATION
         halos.append(
             remote(src.at[pl.ds(0, w)], dst.at[pl.ds(w + rows, w)], halo_send.at[2 * n], halo_recv.at[2 * n], left)
         )
@@ -190,18 +211,26 @@
         c.start()
 
     own_rows = pl.ds(pl.multiple_of(chip * unit, 16), unit)
-    g_ring = (core * side, core * side + 1 + par)
-    g_x = core * side + 2 - par
-
-    def piece(n, g, q):
+    spans = {
+        (d, h): pl.ds(
+            pl.multiple_of(chip_at(on_ring(place - h if d == 0 else place + h), chips) * unit, 16), unit
+        )
+        for d in range(2)
+        for h in range(HOPS + 1)
+    }
+    g_pair = core * side + par
+    g_mid = core * side + 1
+    g_own = core * side + 2 * par
+    g_x = core * side + 2 - 2 * par
+
+    def piece(n, g, many, d, h):
         first, size = PHASES[n]
-        return weights.at[g, pl.ds(first, size), pl.ds(pl.multiple_of(q * unit, 16), unit), :]
-
-    def slot(n, j, d, h):
-        return n * 2 * others + j * others + (h - 1 if d == 0 else HOPS[j][0] + h - 1)
-
-    def origin(d, h):
-        return chip_at(on_ring(place - h if d == 0 else place + h), chips)
+        return weights.at[pl.ds(g, many), pl.ds(first, size), spans[d, h], :]
+
+    def ring_piece(n, d, h, start):
+        if h < HOPS:
+            return piece(n, g_pair, 2, d, start)
+        return piece(n, g_mid if d == 0 else g_own, 1, d, start)
 
     def toward(d):
         q = chip_at(on_ring(place + 1 if d == 0 else place - 1), chips)
@@ -209,44 +238,32 @@
 
     nexts = (toward(0), toward(1))
 
-    def ring_copy(n, j, d, h):
-        q = origin(d, h - 1)
-        p = piece(n, g_ring[j], q)
-        return remote(p, p, bulk_send.at[0], ring_recv.at[slot(n, j, d, h)], nexts[d])
-
-    def ring_wait(n, j, d, h):
-        p = piece(n, g_ring[j], origin(d, h))
-        remote(p, p, bulk_send.at[0], ring_recv.at[slot(n, j, d, h)], nexts[d]).wait_recv()
-
-    def to_twin(n, g, q):
-        p = piece(n, g, q)
+    def ring_copy(n, d, h, start):
+        p = ring_piece(n, d, h, start)
+        return remote(p, p, bulk_send.at[0], ring_recv.at[n * 2 * HOPS + 2 * (h - 1) + d], nexts[d])
+
+    def to_twin(n, p):
         remote(p, p, bulk_send.at[2], core_recv.at[n], twin).start()
 
+    def x_copy(n, d, h, g):
+        p = piece(n, g, 1, d, h)
+        return remote(p, p, bulk_send.at[1], x_recv.at[n * 2 * HOPS + 2 * (h - 1) + d], across)
+
     def hop(n, h):
-        for j in range(2):
-            for d in range(2):
-                if h > HOPS[j][d]:
-                    continue
-                ring_wait(n, j, d, h)
-                if h < HOPS[j][d]:
-                    ring_copy(n, j, d, h + 1).start()
-                q = origin(d, h)
-                if j == 1:
-                    p = piece(n, g_ring[1], q)
-                    remote(p, p, bulk_send.at[1], x_recv.at[n * others + slot(0, 1, d, h) - others], across).start()
-        for j in range(2):
-            for d in range(2):
-                if h <= HOPS[j][d]:
-                    to_twin(n, g_ring[j], origin(d, h))
+        for d in range(2):
+            ring_copy(n, d, h, h).wait_recv()
+            if h < HOPS:
+                ring_copy(n, d, h + 1, h).start()
+            if h < HOPS or d == 1:
+                x_copy(n, d, h, g_own).start()
+        for d in range(2):
+            to_twin(n, ring_piece(n, d, h, h))
 
     def xhop(n, h):
         for d in range(2):
-            if h > HOPS[1][d]:
-                continue
-            q = origin(d, h)
-            p = piece(n, g_x, q)
-            remote(p, p, bulk_send.at[1], x_recv.at[n * others + slot(0, 1, d, h) - others], across).wait_recv()
-            to_twin(n, g_x, q)
+            if h < HOPS or d == 1:
+                x_copy(n, d, h, g_x).wait_recv()
+                to_twin(n, piece(n, g_x, 1, d, h))
 
     def settle(n):
         first, size = PHASES[n]
@@ -262,47 +279,47 @@
         p = remote(wpad.at[mine, pl.ds(*PHASES[n])], wpeer.at[mine, pl.ds(*PHASES[n])], init_send.at[n], init_recv.at[n], twin)
         p.wait_recv()
         assemble(n, core * side)
-        for j in range(2):
-            for d in range(2):
-                ring_copy(n, j, d, 1).start()
+        for d in range(2):
+            ring_copy(n, d, 1, 0).start()
 
     launch(0)
     launch(1)
-    w = DILATION
-    fx[w:w + rows, :] = feats[...]
-    nx[w:w + rows, :] = noise[...]
-    bx[w:w + rows, :] = bottle[...]
-    hop(0, 1)
+    for c in loads:
+        c.wait()
 
     def outer(g):
         cols = pl.ds(pl.multiple_of(g * GROUP, GROUP), GROUP)
-        return lax.dot_general(bottle[...], noise[:, cols], (((0,), (0,)), ((), ())), preferred_element_type=F32)
+        return lax.dot_general(
+            bx[middle, :], nx[middle, cols], (((0,), (0,)), ((), ())), preferred_element_type=F32
+        ).reshape(chips, unit, GROUP)
 
     for g in range(side):
-        csend[:, :, g * GROUP:(g + 1) * GROUP] = outer((1 - core) * side + g).astype(BF16).reshape(chips, unit, GROUP)
+        csend[:, :, g * GROUP:(g + 1) * GROUP] = outer((1 - core) * side + g).astype(BF16)
     rs_core = remote(csend, crecv, rs_send.at[0], rs_recv.at[0], twin)
     rs_core.start()
-    hop(0, 2)
+    hop(0, 1)
     launch(2)
     for g in range(side):
-        keep[:, :, g * GROUP:(g + 1) * GROUP] = outer(core * side + g).reshape(chips, unit, GROUP)
-    hop(0, 3)
+        keep[:, :, g * GROUP:(g + 1) * GROUP] = outer(core * side + g)
+    hop(0, 2)
     xhop(0, 1)
+    hop(1, 1)
     rs_core.wait_recv()
     for z in range(zs):
         ysend[z] = (keep[2 * z + 1 - yy] + crecv[2 * z + 1 - yy].astype(F32)).astype(BF16)
     rs_y = remote(ysend, yrecv, rs_send.at[1], rs_recv.at[1], near_dev(0, 1, 0))
     rs_y.start()
-    hop(0, 4)
+    hop(0, 3)
     xhop(0, 2)
-    hop(1, 1)
-    xhop(0, 3)
-    xhop(0, 4)
     remote(wpad.at[theirs], wpeer.at[theirs], init_send.at[3], init_recv.at[3], twin).wait_recv()
     for n in range(3):
         assemble(n, (1 - core) * side)
-    for c in halos:
-        c.wait()
+    hop(0, 4)
+    xhop(0, 3)
+    hop(1, 2)
+    xhop(0, 4)
+    xhop(1, 1)
+    hop(2, 1)
     rs_y.wait_recv()
     for z in range(zs):
         total = keep[2 * z + yy] + crecv[2 * z + yy].astype(F32) + yrecv[z].astype(F32)
@@ -313,6 +330,8 @@
         c = remote(zsend.at[lax.rem(zz + d, zs)], zrecv.at[d - 1], rs_send.at[1 + d], rs_recv.at[1 + d], line[d - 1])
         c.start()
         rs_z.append(c)
+    for c in halos:
+        c.wait()
     settle(0)
 
     edge = lax.broadcasted_iota(jnp.int32, (rows + 2 * w, 1), 0)
@@ -329,21 +348,20 @@
             act[p, :, cols] = jnp.where(inside, jax.nn.gelu(state), 0.0).astype(BF16)
 
     enter(0)
-    enter(1)
-    hop(1, 2)
-    xhop(1, 1)
-    enter(2)
-    enter(3)
     hop(1, 3)
     xhop(1, 2)
+    enter(1)
+    hop(2, 2)
+    xhop(2, 1)
+    enter(2)
+    hop(1, 4)
+    xhop(1, 3)
+    enter(3)
+    hop(2, 3)
+    xhop(1, 4)
+    xhop(2, 2)
     enter(4)
     enter(5)
-    hop(1, 4)
-    xhop(1, 3)
-    hop(2, 1)
-    xhop(1, 4)
-    hop(2, 2)
-    xhop(2, 1)
     for c in rs_z:
         c.wait_recv()
     owned = keep[chip]
@@ -355,25 +373,21 @@
     rs_x.start()
     settle(1)
 
-    def mix(k, p):
-        total = jnp.zeros((rows, bot), F32)
+    def mix(k):
+        total = jnp.zeros((2 * rows, bot), F32)
         for g in range(groups):
+            left_side = act[:, k * w:k * w + rows, g * GROUP:(g + 1) * GROUP].reshape(2 * rows, GROUP)
             total = total + lax.dot_general(
-                act[p, k * w:k * w + rows, g * GROUP:(g + 1) * GROUP], weights[g, 1 + k],
-                (((1,), (1,)), ((), ())), preferred_element_type=F32,
+                left_side, weights[g, 1 + k], (((1,), (1,)), ((), ())), preferred_element_type=F32
             )
         return total
 
-    def mixed(p):
-        inner[p] = jax.nn.gelu(mix(0, p) + mix(1, p) + mix(2, p)).astype(BF16)
-
-    mixed(0)
-    hop(2, 3)
-    xhop(2, 2)
-    mixed(1)
+    mixed[...] = mix(0)
     hop(2, 4)
     xhop(2, 3)
+    mixed[...] += mix(1)
     xhop(2, 4)
+    inner[...] = jax.nn.gelu(mixed[...] + mix(2)).astype(BF16)
     rs_x.wait_recv()
     pair[1 - par] = xrecv[...].astype(F32)
     give = pl.ds(pl.multiple_of((1 - core) * (unit // 2), 8), unit // 2)
@@ -385,13 +399,14 @@
     lanes = jnp.zeros((1, GROUP), F32)
     for g in range(groups):
         cols = pl.ds(g * GROUP, GROUP)
-        off = noise[:, cols].astype(F32) * NOISE_SCALE
+        off = nx[middle, cols].astype(F32) * NOISE_SCALE
         b = base[:, cols]
-        upper = b + off + jnp.dot(inner[0], weights[g, 4], preferred_element_type=F32)
-        lower = b - off + jnp.dot(inner[1], weights[g, 4], preferred_element_type=F32)
+        outs = jnp.dot(inner[...], weights[g, 4], preferred_element_type=F32)
+        upper = b + off + outs[:rows]
+        lower = b - off + outs[rows:]
         both = upper + lower
         blended[:, cols] = (both * 0.5).astype(BF16)
-        lanes = lanes + jnp.sum((upper - lower) * (both - 2.0 * goal[:, cols].astype(F32)), axis=0, keepdims=True)
+        lanes = lanes + jnp.sum((upper - lower) * (both - 2.0 * gx[:, cols].astype(F32)), axis=0, keepdims=True)
     local = jnp.sum(lanes, axis=1, keepdims=True) / (rows * count * chans)
     shelf = lax.broadcasted_iota(jnp.int32, (8, 128), 0)
     gaps1[0] = jnp.where(shelf == par, local, 0.0)
@@ -435,13 +450,6 @@
     unit = 2 * share
     groups = chans // GROUP
     zs = chips // 2
-    core = lax.axis_index("ctx") % 2
-    shard = jnp.concatenate([entry_weight[None], jnp.swapaxes(conv_filters, 1, 2), exit_weight[None]], axis=0)
-    shard = shard.reshape(5, share, groups, GROUP).transpose(2, 0, 1, 3)
-    none = jnp.zeros_like(shard)
-    wpad = jnp.concatenate(
-        [jnp.where(core == 0, shard, none), jnp.where(core == 1, shard, none)], axis=2
-    )
     wide = rows + 2 * DILATION
     half = chans // 2
     blended, estimate = pl.pallas_call(
@@ -450,17 +458,20 @@
             jax.ShapeDtypeStruct((rows, chans), BF16),
             jax.ShapeDtypeStruct((share, chans), F32),
         ),
-        in_specs=[pl.BlockSpec(memory_space=pltpu.VMEM)] * 5,
+        in_specs=[pl.BlockSpec(memory_space=pl.ANY)] * 4 + [pl.BlockSpec(memory_space=pltpu.VMEM)] * 3,
         out_specs=[pl.BlockSpec(memory_space=pltpu.VMEM)] * 2,
         scratch_shapes=[
             pltpu.VMEM((groups, 5, bot, GROUP), BF16),
             pltpu.VMEM((groups, 5, unit, GROUP), BF16),
+            pltpu.VMEM((groups, 5, unit, GROUP), BF16),
             pltpu.VMEM((wide, chans), BF16),
             pltpu.VMEM((wide, chans), BF16),
             pltpu.VMEM((wide, bot), BF16),
+            pltpu.VMEM((rows, chans), BF16),
             pltpu.VMEM((2, wide, chans), BF16),
             pltpu.VMEM((rows, chans), F32),
-            pltpu.VMEM((2, rows, bot), BF16),
+            pltpu.VMEM((2 * rows, bot), F32),
+            pltpu.VMEM((2 * rows, bot), BF16),
             pltpu.VMEM((chips, unit, half), F32),
             pltpu.VMEM((chips, unit, half), BF16),
             pltpu.VMEM((chips, unit, half), BF16),
@@ -474,8 +485,8 @@
             pltpu.VMEM((2, unit // 2, half), F32),
             pltpu.VMEM((8, 8, 128), F32),
             pltpu.VMEM((zs, 8, 128), F32),
-            pltpu.SemaphoreType.DMA((3 * 2 * (chips - 1),)),
-            pltpu.SemaphoreType.DMA((3 * (chips - 1),)),
+            pltpu.SemaphoreType.DMA((3 * 2 * HOPS,)),
+            pltpu.SemaphoreType.DMA((3 * 2 * HOPS,)),
             pltpu.SemaphoreType.DMA((3,)),
             pltpu.SemaphoreType.DMA((7,)),
             pltpu.SemaphoreType.DMA((4,)),
@@ -484,11 +495,15 @@
             pltpu.SemaphoreType.DMA((6,)),
             pltpu.SemaphoreType.DMA((3 + zs,)),
             pltpu.SemaphoreType.DMA((3 + zs,)),
+            pltpu.SemaphoreType.DMA((4,)),
         ],
         compiler_params=pltpu.CompilerParams(
-            collective_id=0, has_side_effects=True, vmem_limit_bytes=48 * 1024 * 1024
+            collective_id=0, has_side_effects=True, vmem_limit_bytes=60 * 1024 * 1024
         ),
-    )(features[0], bottleneck[0], node_noise[0], targets[0], wpad)
+    )(
+        features[0], bottleneck[0], node_noise[0], targets[0],
+        entry_weight, jnp.swapaxes(conv_filters, 1, 2), exit_weight,
+    )
     return blended[None], estimate
 
 

time: 71.1 us -> 65.1 us (0.916)
  local copies, waits for them, and re-layouts: 5.75 us -> 2.62 us
  Pallas kernels: 64.3 us -> 61.7 us
    pallas_call x1, Pallas kernels: 64.3 us -> 61.7 us  [fused(): pl.pallas_call(functools.partial(kernel, chips), out_shape=(jax.ShapeDtyp...]
    concatenate x3 -> x0, local copies, waits for them, and re-layouts: 1.99 us -> none  [fused(): jnp.concatenate([entry_weight[None], jnp.swapaxes(conv_filters, 1, 2), ex...]
    unnamed x12 -> x4, local copies, waits for them, and re-layouts: 3.76 us -> 2.62 us
where the time goes in v2:
time: 65.1 us; the launch traced here: 64.9 us
  Pallas kernels  61.7 us (95%)
  local copies, waits for them, and re-layouts  2.62 us (4%)
    pallas_call x1, Pallas kernels, fused(): pl.pallas_call(functools.partial(kernel, chips), out_shape=(jax.ShapeDtyp...  61.7 us
    unnamed x4, local copies, waits for them, and re-layouts  2.62 us

profile of v2, /device:TPU:0, one launch (start us, length us, event | category | flops | bytes accessed | tf_op | source)
XLA Modules:
  0.0 64.9 jit_solution(5039490542567479070)
XLA Ops:
  0.6 61.7 %shard_map.86 = (bf16[192,1536]{1,0:T(8,128)(2,1)}, f32[24,1536]{1,0:T(8,128)}) custom-call(bf16[192,1536]{1,0:T(8,128)(2,1)} %bitcast.7, bf16[192,384]{1,0:T(8,128)(2,1)} %bitcast.11, bf16[192,1536]{1,0:T(8,128)(2,1)} %bitcast.8, bf16[192,1536]{1,0:T(8,128)(2,1)} %bitcast.9, bf16[24,1536]{1,0:T(8,128)(2,1)} %entry.1, bf16[3,24,1536]{2,1,0:T(8,128)(2,1)} %bitcast.10, ...), custom_call_target="tpu_custom_call" | custom-call | tf_op jit(solution)/shard_map/pallas_call | solution.py:455
  62.3 0.0 copy-start
  62.3 2.0 %copy.11 = bf16[1,192,1536]{2,1,0:T(8,128)(2,1)} copy(bf16[1,192,1536]{2,1,0:T(8,128)(2,1)} %bitcast.6) | data formatting | bytes 1179648
  64.3 0.0 copy-done
  64.3 0.7 %copy.12 = f32[24,1536]{1,0:T(8,128)} copy(f32[24,1536]{1,0:T(8,128)S(1)} %copy-done) | data formatting | bytes 294912
Async XLA Ops:
  62.3 2.0 %copy-start = (f32[24,1536]{1,0:T(8,128)S(1)}, f32[24,1536]{1,0:T(8,128)}, u32[]{:S(2)}) copy-start(f32[24,1536]{1,0:T(8,128)} %get-tuple-element.9) | copy-start | bytes 442372

commit v3 on v2

--- a/solution.py
+++ b/solution.py
@@ -93,6 +93,7 @@
 GROUP = 256
 PHASES = ((0, 1), (1, 3), (4, 1))
 HOPS = 4
+EARLY = 2
 
 
 def chip_at(position, chips):
@@ -103,7 +104,7 @@
     chips,
     feats, bottle, noise, goal, entry, filters, leave,
     blended, estimate,
-    weights, wpad, wpeer, fx, nx, bx, gx, act, base, mixed, inner,
+    weights, wpad, wpeer, fx, nx, bx, bo, gx, act, base, mixed, inner, mixed_late, inner_late,
     keep, csend, crecv, ysend, yrecv, zsend, zrecv, xsend, xrecv, pair, prow, gaps1, gaps2,
     ring_recv, x_recv, core_recv, bulk_send, init_send, init_recv, halo_send, halo_recv, rs_send, rs_recv, load,
 ):
@@ -199,25 +200,42 @@
     inits.append(remote(wpad.at[mine], wpeer.at[mine], init_send.at[3], init_recv.at[3], twin))
     for c in inits:
         c.start()
-    halos = []
+    to_left = []
+    to_right = []
     for n, (src, dst) in enumerate(((feats, fx), (noise, nx), (bottle, bx))):
-        halos.append(
+        to_left.append(
             remote(src.at[pl.ds(0, w)], dst.at[pl.ds(w + rows, w)], halo_send.at[2 * n], halo_recv.at[2 * n], left)
         )
-        halos.append(
+        to_right.append(
             remote(src.at[pl.ds(rows - w, w)], dst.at[pl.ds(0, w)], halo_send.at[2 * n + 1], halo_recv.at[2 * n + 1], right)
         )
-    for c in halos:
-        c.start()
-
-    own_rows = pl.ds(pl.multiple_of(chip * unit, 16), unit)
-    spans = {
-        (d, h): pl.ds(
-            pl.multiple_of(chip_at(on_ring(place - h if d == 0 else place + h), chips) * unit, 16), unit
-        )
-        for d in range(2)
-        for h in range(HOPS + 1)
-    }
+
+    @pl.when(ctx > 0)
+    def _():
+        for c in to_left:
+            c.start()
+
+    @pl.when(ctx < count - 1)
+    def _():
+        for c in to_right:
+            c.start()
+
+    @pl.when(ctx == 0)
+    def _():
+        for dst in (fx, nx, bx):
+            dst[0:w, :] = jnp.zeros((w, dst.shape[1]), BF16)
+
+    @pl.when(ctx == count - 1)
+    def _():
+        for dst in (fx, nx, bx):
+            dst[w + rows:, :] = jnp.zeros((w, dst.shape[1]), BF16)
+
+    def span(d, h):
+        return pl.ds(unit * (0 if h == 0 else min(2 * h - 1 + d, chips - 1)), unit)
+
+    def chip_of(k):
+        return chip_at(on_ring(place if k == 0 else place - (k + 1) // 2 if k % 2 else place + k // 2), chips)
+
     g_pair = core * side + par
     g_mid = core * side + 1
     g_own = core * side + 2 * par
@@ -225,7 +243,7 @@
 
     def piece(n, g, many, d, h):
         first, size = PHASES[n]
-        return weights.at[pl.ds(g, many), pl.ds(first, size), spans[d, h], :]
+        return weights.at[pl.ds(g, many), pl.ds(first, size), span(d, h), :]
 
     def ring_piece(n, d, h, start):
         if h < HOPS:
@@ -238,12 +256,12 @@
 
     nexts = (toward(0), toward(1))
 
-    def ring_copy(n, d, h, start):
-        p = ring_piece(n, d, h, start)
-        return remote(p, p, bulk_send.at[0], ring_recv.at[n * 2 * HOPS + 2 * (h - 1) + d], nexts[d])
-
-    def to_twin(n, p):
-        remote(p, p, bulk_send.at[2], core_recv.at[n], twin).start()
+    def ring_copy(n, d, h):
+        return remote(ring_piece(n, d, h, h - 1), ring_piece(n, d, h, h), bulk_send.at[0], ring_recv.at[n * 2 * HOPS + 2 * (h - 1) + d], nexts[d])
+
+    def to_twin(n, h, p):
+        late = 1 if n == 1 and h > EARLY else 0
+        remote(p, p, bulk_send.at[2], core_recv.at[n + 2 * late], twin).start()
 
     def x_copy(n, d, h, g):
         p = piece(n, g, 1, d, h)
@@ -251,36 +269,36 @@
 
     def hop(n, h):
         for d in range(2):
-            ring_copy(n, d, h, h).wait_recv()
+            ring_copy(n, d, h).wait_recv()
             if h < HOPS:
-                ring_copy(n, d, h + 1, h).start()
+                ring_copy(n, d, h + 1).start()
             if h < HOPS or d == 1:
                 x_copy(n, d, h, g_own).start()
         for d in range(2):
-            to_twin(n, ring_piece(n, d, h, h))
+            to_twin(n, h, ring_piece(n, d, h, h))
 
     def xhop(n, h):
         for d in range(2):
             if h < HOPS or d == 1:
                 x_copy(n, d, h, g_x).wait_recv()
-                to_twin(n, piece(n, g_x, 1, d, h))
-
-    def settle(n):
+                to_twin(n, h, piece(n, g_x, 1, d, h))
+
+    def settle(n, sem, blocks):
         first, size = PHASES[n]
-        drain(weights.at[pl.ds(0, side), pl.ds(first, size), pl.ds(0, others * unit)], core_recv.at[n])
+        drain(weights.at[pl.ds(0, side), pl.ds(first, size), pl.ds(0, blocks * unit)], core_recv.at[sem])
 
     def assemble(n, begin):
         first, size = PHASES[n]
         for g in range(side):
             for m in range(first, first + size):
-                weights[begin + g, m, own_rows, :] = wpad[begin + g, m] + wpeer[begin + g, m]
+                weights[begin + g, m, 0:unit, :] = wpad[begin + g, m] + wpeer[begin + g, m]
 
     def launch(n):
         p = remote(wpad.at[mine, pl.ds(*PHASES[n])], wpeer.at[mine, pl.ds(*PHASES[n])], init_send.at[n], init_recv.at[n], twin)
         p.wait_recv()
         assemble(n, core * side)
         for d in range(2):
-            ring_copy(n, d, 1, 0).start()
+            ring_copy(n, d, 1).start()
 
     launch(0)
     launch(1)
@@ -330,9 +348,26 @@
         c = remote(zsend.at[lax.rem(zz + d, zs)], zrecv.at[d - 1], rs_send.at[1 + d], rs_recv.at[1 + d], line[d - 1])
         c.start()
         rs_z.append(c)
-    for c in halos:
-        c.wait()
-    settle(0)
+
+    @pl.when(ctx > 0)
+    def _():
+        for n in range(3):
+            to_left[n].wait_send()
+            to_right[n].wait_recv()
+
+    @pl.when(ctx < count - 1)
+    def _():
+        for n in range(3):
+            to_right[n].wait_send()
+            to_left[n].wait_recv()
+
+    order = lax.broadcasted_iota(jnp.int32, (bot, bot), 1)
+    wanted = order
+    for k in range(chips):
+        wanted = jnp.where(order >= k * unit, order + (chip_of(k) - k) * unit, wanted)
+    swap = jnp.where(lax.broadcasted_iota(jnp.int32, (bot, bot), 0) == wanted, 1.0, 0.0).astype(BF16)
+    bo[...] = jnp.dot(bx[...], swap, preferred_element_type=F32).astype(BF16)
+    settle(0, 0, others)
 
     edge = lax.broadcasted_iota(jnp.int32, (rows + 2 * w, 1), 0)
     inside = jnp.logical_and(
@@ -341,7 +376,7 @@
 
     def enter(g):
         cols = pl.ds(g * GROUP, GROUP)
-        b = fx[:, cols].astype(F32) + jnp.dot(bx[...], weights[g, 0], preferred_element_type=F32)
+        b = fx[:, cols].astype(F32) + jnp.dot(bo[...], weights[g, 0], preferred_element_type=F32)
         off = nx[:, cols].astype(F32) * NOISE_SCALE
         base[:, cols] = b[w:w + rows]
         for p, state in enumerate((b + off, b - off)):
@@ -354,14 +389,31 @@
     hop(2, 2)
     xhop(2, 1)
     enter(2)
+    enter(3)
     hop(1, 4)
     xhop(1, 3)
-    enter(3)
+    enter(4)
+    enter(5)
     hop(2, 3)
     xhop(1, 4)
     xhop(2, 2)
-    enter(4)
-    enter(5)
+    soon = (2 * EARLY + 1) * unit
+    settle(1, 1, 2 * EARLY)
+
+    def mix(k, begin, size):
+        total = jnp.zeros((2 * rows, size), F32)
+        for g in range(groups):
+            left_side = act[:, k * w:k * w + rows, g * GROUP:(g + 1) * GROUP].reshape(2 * rows, GROUP)
+            total = total + lax.dot_general(
+                left_side, weights[g, 1 + k, begin:begin + size, :],
+                (((1,), (1,)), ((), ())), preferred_element_type=F32,
+            )
+        return total
+
+    mixed[...] = mix(0, 0, soon)
+    hop(2, 4)
+    xhop(2, 3)
+    mixed[...] += mix(1, 0, soon)
     for c in rs_z:
         c.wait_recv()
     owned = keep[chip]
@@ -371,37 +423,27 @@
     xsend[...] = owned.astype(BF16)
     rs_x = remote(xsend, xrecv, rs_send.at[1 + zs], rs_recv.at[1 + zs], across)
     rs_x.start()
-    settle(1)
-
-    def mix(k):
-        total = jnp.zeros((2 * rows, bot), F32)
-        for g in range(groups):
-            left_side = act[:, k * w:k * w + rows, g * GROUP:(g + 1) * GROUP].reshape(2 * rows, GROUP)
-            total = total + lax.dot_general(
-                left_side, weights[g, 1 + k], (((1,), (1,)), ((), ())), preferred_element_type=F32
-            )
-        return total
-
-    mixed[...] = mix(0)
-    hop(2, 4)
-    xhop(2, 3)
-    mixed[...] += mix(1)
     xhop(2, 4)
-    inner[...] = jax.nn.gelu(mixed[...] + mix(2)).astype(BF16)
+    inner[...] = jax.nn.gelu(mixed[...] + mix(2, 0, soon)).astype(BF16)
+    settle(1, 3, others - 2 * EARLY)
+    mixed_late[...] = mix(0, soon, bot - soon)
+    mixed_late[...] += mix(1, soon, bot - soon)
+    inner_late[...] = jax.nn.gelu(mixed_late[...] + mix(2, soon, bot - soon)).astype(BF16)
     rs_x.wait_recv()
     pair[1 - par] = xrecv[...].astype(F32)
     give = pl.ds(pl.multiple_of((1 - core) * (unit // 2), 8), unit // 2)
     have = pl.ds(pl.multiple_of(core * (unit // 2), 8), unit // 2)
     rs_f = remote(pair.at[:, give, :], prow, rs_send.at[2 + zs], rs_recv.at[2 + zs], twin)
     rs_f.start()
-    settle(2)
+    settle(2, 2, others)
 
     lanes = jnp.zeros((1, GROUP), F32)
     for g in range(groups):
         cols = pl.ds(g * GROUP, GROUP)
         off = nx[middle, cols].astype(F32) * NOISE_SCALE
         b = base[:, cols]
-        outs = jnp.dot(inner[...], weights[g, 4], preferred_element_type=F32)
+        outs = jnp.dot(inner[...], weights[g, 4, 0:soon, :], preferred_element_type=F32)
+        outs = outs + jnp.dot(inner_late[...], weights[g, 4, soon:bot, :], preferred_element_type=F32)
         upper = b + off + outs[:rows]
         lower = b - off + outs[rows:]
         both = upper + lower
@@ -452,13 +494,14 @@
     zs = chips // 2
     wide = rows + 2 * DILATION
     half = chans // 2
+    soon = (2 * EARLY + 1) * unit
     blended, estimate = pl.pallas_call(
         functools.partial(kernel, chips),
         out_shape=(
             jax.ShapeDtypeStruct((rows, chans), BF16),
             jax.ShapeDtypeStruct((share, chans), F32),
         ),
-        in_specs=[pl.BlockSpec(memory_space=pl.ANY)] * 4 + [pl.BlockSpec(memory_space=pltpu.VMEM)] * 3,
+        in_specs=[pl.BlockSpec(memory_space=pltpu.HBM)] * 4 + [pl.BlockSpec(memory_space=pltpu.VMEM)] * 3,
         out_specs=[pl.BlockSpec(memory_space=pltpu.VMEM)] * 2,
         scratch_shapes=[
             pltpu.VMEM((groups, 5, bot, GROUP), BF16),
@@ -467,11 +510,14 @@
             pltpu.VMEM((wide, chans), BF16),
             pltpu.VMEM((wide, chans), BF16),
             pltpu.VMEM((wide, bot), BF16),
+            pltpu.VMEM((wide, bot), BF16),
             pltpu.VMEM((rows, chans), BF16),
             pltpu.VMEM((2, wide, chans), BF16),
             pltpu.VMEM((rows, chans), F32),
-            pltpu.VMEM((2 * rows, bot), F32),
-            pltpu.VMEM((2 * rows, bot), BF16),
+            pltpu.VMEM((2 * rows, soon), F32),
+            pltpu.VMEM((2 * rows, soon), BF16),
+            pltpu.VMEM((2 * rows, bot - soon), F32),
+            pltpu.VMEM((2 * rows, bot - soon), BF16),
             pltpu.VMEM((chips, unit, half), F32),
             pltpu.VMEM((chips, unit, half), BF16),
             pltpu.VMEM((chips, unit, half), BF16),
@@ -487,7 +533,7 @@
             pltpu.VMEM((zs, 8, 128), F32),
             pltpu.SemaphoreType.DMA((3 * 2 * HOPS,)),
             pltpu.SemaphoreType.DMA((3 * 2 * HOPS,)),
-            pltpu.SemaphoreType.DMA((3,)),
+            pltpu.SemaphoreType.DMA((4,)),
             pltpu.SemaphoreType.DMA((7,)),
             pltpu.SemaphoreType.DMA((4,)),
             pltpu.SemaphoreType.DMA((4,)),
@@ -498,7 +544,7 @@
             pltpu.SemaphoreType.DMA((4,)),
         ],
         compiler_params=pltpu.CompilerParams(
-            collective_id=0, has_side_effects=True, vmem_limit_bytes=60 * 1024 * 1024
+            collective_id=0, has_side_effects=True, vmem_limit_bytes=59 * 1024 * 1024
         ),
     )(
         features[0], bottleneck[0], node_noise[0], targets[0],

time: 65.1 us -> 64.7 us (level)
  no operation moved by 1% of the time
where the time goes in v3:
time: 64.7 us; the launch traced here: 64.5 us
  Pallas kernels  61.3 us (95%)
  local copies, waits for them, and re-layouts  2.62 us (4%)
  between operations  0.65 us (1%)
    pallas_call x1, Pallas kernels, fused(): pl.pallas_call(functools.partial(kernel, chips), out_shape=(jax.ShapeDtyp...  61.3 us
    unnamed x4, local copies, waits for them, and re-layouts  2.62 us

profile of v3, /device:TPU:0, one launch (start us, length us, event | category | flops | bytes accessed | tf_op | source)
XLA Modules:
  0.0 64.5 jit_solution(13745338285766912019)
XLA Ops:
  0.6 61.3 %shard_map.86 = (bf16[192,1536]{1,0:T(8,128)(2,1)}, f32[24,1536]{1,0:T(8,128)}) custom-call(bf16[192,1536]{1,0:T(8,128)(2,1)} %bitcast.7, bf16[192,384]{1,0:T(8,128)(2,1)} %bitcast.11, bf16[192,1536]{1,0:T(8,128)(2,1)} %bitcast.8, bf16[192,1536]{1,0:T(8,128)(2,1)} %bitcast.9, bf16[24,1536]{1,0:T(8,128)(2,1)} %entry.1, bf16[3,24,1536]{2,1,0:T(8,128)(2,1)} %bitcast.10, ...), custom_call_target="tpu_custom_call" | custom-call | tf_op jit(solution)/shard_map/pallas_call | solution.py:498
  61.9 0.0 copy-start
  61.9 2.0 %copy.11 = bf16[1,192,1536]{2,1,0:T(8,128)(2,1)} copy(bf16[1,192,1536]{2,1,0:T(8,128)(2,1)} %bitcast.6) | data formatting | bytes 1179648
  63.9 0.0 copy-done
  63.9 0.7 %copy.12 = f32[24,1536]{1,0:T(8,128)} copy(f32[24,1536]{1,0:T(8,128)S(1)} %copy-done) | data formatting | bytes 294912
Async XLA Ops:
  61.9 2.0 %copy-start = (f32[24,1536]{1,0:T(8,128)S(1)}, f32[24,1536]{1,0:T(8,128)}, u32[]{:S(2)}) copy-start(f32[24,1536]{1,0:T(8,128)} %get-tuple-element.9) | copy-start | bytes 442372

commit v4 on v3

--- a/solution.py
+++ b/solution.py
@@ -92,12 +92,6 @@
 BF16 = jnp.bfloat16
 GROUP = 256
 PHASES = ((0, 1), (1, 3), (4, 1))
-HOPS = 4
-EARLY = 2
-
-
-def chip_at(position, chips):
-    return jnp.where(position < chips // 2, 2 * position, 2 * (chips - 1 - position) + 1)
 
 
 def kernel(
@@ -126,13 +120,9 @@
     zz = chip // 2
     par = lax.rem(dp, 2)
     mate = dp + 1 - 2 * par
-    place = jnp.where(yy == 0, zz, chips - 1 - zz)
 
     def at(d, z, y, c):
         return {"dp": d, "ctx": (z * 2 + y) * 2 + c}
-
-    def on_ring(p):
-        return lax.rem(p + chips, chips)
 
     twin = at(dp, zz, yy, 1 - core)
     across = at(mate, zz, yy, core)
@@ -163,6 +153,9 @@
     ]
     for c in loads:
         c.start()
+    barrier = pltpu.get_barrier_semaphore()
+    for peer in peers:
+        pl.semaphore_signal(barrier, inc=1, device_id=peer, device_id_type=pl.DeviceIdType.MESH)
     blank = jnp.zeros((share, GROUP), F32)
     for g in range(groups):
         for m in range(5):
@@ -171,10 +164,6 @@
             low = jnp.concatenate([part, blank], axis=0)
             high = jnp.concatenate([blank, part], axis=0)
             wpad[g, m] = jnp.where(core == 0, low, high).astype(BF16)
-
-    barrier = pltpu.get_barrier_semaphore()
-    for peer in peers:
-        pl.semaphore_signal(barrier, inc=1, device_id=peer, device_id_type=pl.DeviceIdType.MESH)
     pl.semaphore_wait(barrier, len(peers))
 
     def remote(src, dst, ssem, rsem, dev):
@@ -230,58 +219,48 @@
         for dst in (fx, nx, bx):
             dst[w + rows:, :] = jnp.zeros((w, dst.shape[1]), BF16)
 
-    def span(d, h):
-        return pl.ds(unit * (0 if h == 0 else min(2 * h - 1 + d, chips - 1)), unit)
-
     def chip_of(k):
-        return chip_at(on_ring(place if k == 0 else place - (k + 1) // 2 if k % 2 else place + k // 2), chips)
+        return lax.rem(zz + zs - k % zs, zs) * 2 + (yy if k < zs else 1 - yy)
 
     g_pair = core * side + par
     g_mid = core * side + 1
     g_own = core * side + 2 * par
     g_x = core * side + 2 - 2 * par
 
-    def piece(n, g, many, d, h):
+    def piece(n, g, many, k):
         first, size = PHASES[n]
-        return weights.at[pl.ds(g, many), pl.ds(first, size), span(d, h), :]
-
-    def ring_piece(n, d, h, start):
-        if h < HOPS:
-            return piece(n, g_pair, 2, d, start)
-        return piece(n, g_mid if d == 0 else g_own, 1, d, start)
-
-    def toward(d):
-        q = chip_at(on_ring(place + 1 if d == 0 else place - 1), chips)
-        return {"dp": dp, "ctx": q * 2 + core}
-
-    nexts = (toward(0), toward(1))
-
-    def ring_copy(n, d, h):
-        return remote(ring_piece(n, d, h, h - 1), ring_piece(n, d, h, h), bulk_send.at[0], ring_recv.at[n * 2 * HOPS + 2 * (h - 1) + d], nexts[d])
-
-    def to_twin(n, h, p):
-        late = 1 if n == 1 and h > EARLY else 0
+        return weights.at[pl.ds(g, many), pl.ds(first, size), pl.ds(k * unit, unit), :]
+
+    beside = near_dev(0, 1, 0)
+
+    def plane_copy(n, k):
+        dst = piece(n, g_pair, 2, k)
+        src = piece(n, g_pair, 2, 0 if k < zs else k - zs)
+        return remote(src, dst, bulk_send.at[0], ring_recv.at[n * others + k - 1], line[k - 1] if k < zs else beside)
+
+    def to_twin(n, k, p):
+        late = 1 if n == 1 and k > zs else 0
         remote(p, p, bulk_send.at[2], core_recv.at[n + 2 * late], twin).start()
 
-    def x_copy(n, d, h, g):
-        p = piece(n, g, 1, d, h)
-        return remote(p, p, bulk_send.at[1], x_recv.at[n * 2 * HOPS + 2 * (h - 1) + d], across)
-
-    def hop(n, h):
-        for d in range(2):
-            ring_copy(n, d, h).wait_recv()
-            if h < HOPS:
-                ring_copy(n, d, h + 1).start()
-            if h < HOPS or d == 1:
-                x_copy(n, d, h, g_own).start()
-        for d in range(2):
-            to_twin(n, h, ring_piece(n, d, h, h))
-
-    def xhop(n, h):
-        for d in range(2):
-            if h < HOPS or d == 1:
-                x_copy(n, d, h, g_x).wait_recv()
-                to_twin(n, h, piece(n, g_x, 1, d, h))
+    def x_copy(n, k, g):
+        p = piece(n, g, 1, k)
+        return remote(p, p, bulk_send.at[1], x_recv.at[n * others + k - 1], across)
+
+    def hop(n, ks):
+        for k in ks:
+            plane_copy(n, k).wait_recv()
+            if k < zs:
+                plane_copy(n, k + zs).start()
+            x_copy(n, k, g_own).start()
+            to_twin(n, k, piece(n, g_pair, 2, k))
+
+    def xhop(n, ks):
+        for k in ks:
+            x_copy(n, k, g_x).wait_recv()
+            to_twin(n, k, piece(n, g_x, 1, k))
+
+    first_half = range(1, zs + 1)
+    last_half = range(zs + 1, chips)
 
     def settle(n, sem, blocks):
         first, size = PHASES[n]
@@ -297,8 +276,8 @@
         p = remote(wpad.at[mine, pl.ds(*PHASES[n])], wpeer.at[mine, pl.ds(*PHASES[n])], init_send.at[n], init_recv.at[n], twin)
         p.wait_recv()
         assemble(n, core * side)
-        for d in range(2):
-            ring_copy(n, d, 1).start()
+        for k in range(1, zs + 1):
+            plane_copy(n, k).start()
 
     launch(0)
     launch(1)
@@ -315,29 +294,62 @@
         csend[:, :, g * GROUP:(g + 1) * GROUP] = outer((1 - core) * side + g).astype(BF16)
     rs_core = remote(csend, crecv, rs_send.at[0], rs_recv.at[0], twin)
     rs_core.start()
-    hop(0, 1)
     launch(2)
+    hop(0, first_half)
     for g in range(side):
         keep[:, :, g * GROUP:(g + 1) * GROUP] = outer(core * side + g)
-    hop(0, 2)
-    xhop(0, 1)
-    hop(1, 1)
+    hop(0, last_half)
+    xhop(0, first_half)
     rs_core.wait_recv()
     for z in range(zs):
         ysend[z] = (keep[2 * z + 1 - yy] + crecv[2 * z + 1 - yy].astype(F32)).astype(BF16)
     rs_y = remote(ysend, yrecv, rs_send.at[1], rs_recv.at[1], near_dev(0, 1, 0))
     rs_y.start()
-    hop(0, 3)
-    xhop(0, 2)
     remote(wpad.at[theirs], wpeer.at[theirs], init_send.at[3], init_recv.at[3], twin).wait_recv()
     for n in range(3):
         assemble(n, (1 - core) * side)
-    hop(0, 4)
-    xhop(0, 3)
-    hop(1, 2)
-    xhop(0, 4)
-    xhop(1, 1)
-    hop(2, 1)
+    xhop(0, last_half)
+
+    @pl.when(ctx > 0)
+    def _():
+        for n in range(3):
+            to_left[n].wait_send()
+            to_right[n].wait_recv()
+
+    @pl.when(ctx < count - 1)
+    def _():
+        for n in range(3):
+            to_right[n].wait_send()
+            to_left[n].wait_recv()
+
+    order = lax.broadcasted_iota(jnp.int32, (bot, bot), 1)
+    wanted = order
+    for k in range(chips):
+        wanted = jnp.where(order >= k * unit, order + (chip_of(k) - k) * unit, wanted)
+    swap = jnp.where(lax.broadcasted_iota(jnp.int32, (bot, bot), 0) == wanted, 1.0, 0.0).astype(BF16)
+    bo[...] = jnp.dot(bx[...], swap, preferred_element_type=F32).astype(BF16)
+    settle(0, 0, others)
+
+    edge = lax.broadcasted_iota(jnp.int32, (rows + 2 * w, 1), 0)
+    inside = jnp.logical_and(
+        jnp.logical_or(edge >= w, ctx > 0), jnp.logical_or(edge < w + rows, ctx < count - 1)
+    )
+
+    def enter(g):
+        cols = pl.ds(g * GROUP, GROUP)
+        b = fx[:, cols].astype(F32) + jnp.dot(bo[...], weights[g, 0], preferred_element_type=F32)
+        off = nx[:, cols].astype(F32) * NOISE_SCALE
+        base[:, cols] = b[w:w + rows]
+        for p, state in enumerate((b + off, b - off)):
+            act[p, :, cols] = jnp.where(inside, jax.nn.gelu(state), 0.0).astype(BF16)
+
+    enter(0)
+    hop(1, range(1, 2))
+    enter(1)
+    hop(1, range(2, 3))
+    enter(2)
+    hop(1, range(3, zs + 1))
+    enter(3)
     rs_y.wait_recv()
     for z in range(zs):
         total = keep[2 * z + yy] + crecv[2 * z + yy].astype(F32) + yrecv[z].astype(F32)
@@ -348,57 +360,13 @@
         c = remote(zsend.at[lax.rem(zz + d, zs)], zrecv.at[d - 1], rs_send.at[1 + d], rs_recv.at[1 + d], line[d - 1])
         c.start()
         rs_z.append(c)
-
-    @pl.when(ctx > 0)
-    def _():
-        for n in range(3):
-            to_left[n].wait_send()
-            to_right[n].wait_recv()
-
-    @pl.when(ctx < count - 1)
-    def _():
-        for n in range(3):
-            to_right[n].wait_send()
-            to_left[n].wait_recv()
-
-    order = lax.broadcasted_iota(jnp.int32, (bot, bot), 1)
-    wanted = order
-    for k in range(chips):
-        wanted = jnp.where(order >= k * unit, order + (chip_of(k) - k) * unit, wanted)
-    swap = jnp.where(lax.broadcasted_iota(jnp.int32, (bot, bot), 0) == wanted, 1.0, 0.0).astype(BF16)
-    bo[...] = jnp.dot(bx[...], swap, preferred_element_type=F32).astype(BF16)
-    settle(0, 0, others)
-
-    edge = lax.broadcasted_iota(jnp.int32, (rows + 2 * w, 1), 0)
-    inside = jnp.logical_and(
-        jnp.logical_or(edge >= w, ctx > 0), jnp.logical_or(edge < w + rows, ctx < count - 1)
-    )
-
-    def enter(g):
-        cols = pl.ds(g * GROUP, GROUP)
-        b = fx[:, cols].astype(F32) + jnp.dot(bo[...], weights[g, 0], preferred_element_type=F32)
-        off = nx[:, cols].astype(F32) * NOISE_SCALE
-        base[:, cols] = b[w:w + rows]
-        for p, state in enumerate((b + off, b - off)):
-            act[p, :, cols] = jnp.where(inside, jax.nn.gelu(state), 0.0).astype(BF16)
-
-    enter(0)
-    hop(1, 3)
-    xhop(1, 2)
-    enter(1)
-    hop(2, 2)
-    xhop(2, 1)
-    enter(2)
-    enter(3)
-    hop(1, 4)
-    xhop(1, 3)
+    hop(2, first_half)
+    xhop(1, first_half)
     enter(4)
     enter(5)
-    hop(2, 3)
-    xhop(1, 4)
-    xhop(2, 2)
-    soon = (2 * EARLY + 1) * unit
-    settle(1, 1, 2 * EARLY)
+    hop(1, last_half)
+    soon = (zs + 1) * unit
+    settle(1, 1, zs)
 
     def mix(k, begin, size):
         total = jnp.zeros((2 * rows, size), F32)
@@ -411,8 +379,9 @@
         return total
 
     mixed[...] = mix(0, 0, soon)
-    hop(2, 4)
-    xhop(2, 3)
+    hop(2, last_half)
+    xhop(1, last_half)
+    xhop(2, first_half)
     mixed[...] += mix(1, 0, soon)
     for c in rs_z:
         c.wait_recv()
@@ -423,9 +392,9 @@
     xsend[...] = owned.astype(BF16)
     rs_x = remote(xsend, xrecv, rs_send.at[1 + zs], rs_recv.at[1 + zs], across)
     rs_x.start()
-    xhop(2, 4)
+    xhop(2, last_half)
     inner[...] = jax.nn.gelu(mixed[...] + mix(2, 0, soon)).astype(BF16)
-    settle(1, 3, others - 2 * EARLY)
+    settle(1, 3, others - zs)
     mixed_late[...] = mix(0, soon, bot - soon)
     mixed_late[...] += mix(1, soon, bot - soon)
     inner_late[...] = jax.nn.gelu(mixed_late[...] + mix(2, soon, bot - soon)).astype(BF16)
@@ -494,7 +463,7 @@
     zs = chips // 2
     wide = rows + 2 * DILATION
     half = chans // 2
-    soon = (2 * EARLY + 1) * unit
+    soon = (zs + 1) * unit
     blended, estimate = pl.pallas_call(
         functools.partial(kernel, chips),
         out_shape=(
@@ -531,8 +500,8 @@
             pltpu.VMEM((2, unit // 2, half), F32),
             pltpu.VMEM((8, 8, 128), F32),
             pltpu.VMEM((zs, 8, 128), F32),
-            pltpu.SemaphoreType.DMA((3 * 2 * HOPS,)),
-            pltpu.SemaphoreType.DMA((3 * 2 * HOPS,)),
+            pltpu.SemaphoreType.DMA((3 * (chips - 1),)),
+            pltpu.SemaphoreType.DMA((3 * (chips - 1),)),
             pltpu.SemaphoreType.DMA((4,)),
             pltpu.SemaphoreType.DMA((7,)),
             pltpu.SemaphoreType.DMA((4,)),

time: 64.7 us -> 64.8 us (level)
  no operation moved by 1% of the time
where the time goes in v4:
time: 64.8 us; the launch traced here: 64.6 us
  Pallas kernels  61.4 us (95%)
  local copies, waits for them, and re-layouts  2.62 us (4%)
  between operations  0.65 us (1%)
    pallas_call x1, Pallas kernels, fused(): pl.pallas_call(functools.partial(kernel, chips), out_shape=(jax.ShapeDtyp...  61.4 us
    unnamed x4, local copies, waits for them, and re-layouts  2.62 us

profile of v4, /device:TPU:0, one launch (start us, length us, event | category | flops | bytes accessed | tf_op | source)
XLA Modules:
  0.0 64.6 jit_solution(6738695284855886557)
XLA Ops:
  0.6 61.4 %shard_map.86 = (bf16[192,1536]{1,0:T(8,128)(2,1)}, f32[24,1536]{1,0:T(8,128)}) custom-call(bf16[192,1536]{1,0:T(8,128)(2,1)} %bitcast.7, bf16[192,384]{1,0:T(8,128)(2,1)} %bitcast.11, bf16[192,1536]{1,0:T(8,128)(2,1)} %bitcast.8, bf16[192,1536]{1,0:T(8,128)(2,1)} %bitcast.9, bf16[24,1536]{1,0:T(8,128)(2,1)} %entry.1, bf16[3,24,1536]{2,1,0:T(8,128)(2,1)} %bitcast.10, ...), custom_call_target="tpu_custom_call" | custom-call | tf_op jit(solution)/shard_map/pallas_call | solution.py:467
  62.0 0.0 copy-start
  62.0 2.0 %copy.11 = bf16[1,192,1536]{2,1,0:T(8,128)(2,1)} copy(bf16[1,192,1536]{2,1,0:T(8,128)(2,1)} %bitcast.6) | data formatting | bytes 1179648
  64.0 0.0 copy-done
  64.0 0.7 %copy.12 = f32[24,1536]{1,0:T(8,128)} copy(f32[24,1536]{1,0:T(8,128)S(1)} %copy-done) | data formatting | bytes 294912
Async XLA Ops:
  62.0 2.0 %copy-start = (f32[24,1536]{1,0:T(8,128)S(1)}, f32[24,1536]{1,0:T(8,128)}, u32[]{:S(2)}) copy-start(f32[24,1536]{1,0:T(8,128)} %get-tuple-element.9) | copy-start | bytes 442372

commit v5 on v4

--- a/solution.py
+++ b/solution.py
@@ -227,9 +227,9 @@
     g_own = core * side + 2 * par
     g_x = core * side + 2 - 2 * par
 
-    def piece(n, g, many, k):
+    def piece(n, g, many, k, blocks=1):
         first, size = PHASES[n]
-        return weights.at[pl.ds(g, many), pl.ds(first, size), pl.ds(k * unit, unit), :]
+        return weights.at[pl.ds(g, many), pl.ds(first, size), pl.ds(k * unit, blocks * unit), :]
 
     beside = near_dev(0, 1, 0)
 
@@ -238,29 +238,30 @@
         src = piece(n, g_pair, 2, 0 if k < zs else k - zs)
         return remote(src, dst, bulk_send.at[0], ring_recv.at[n * others + k - 1], line[k - 1] if k < zs else beside)
 
-    def to_twin(n, k, p):
-        late = 1 if n == 1 and k > zs else 0
-        remote(p, p, bulk_send.at[2], core_recv.at[n + 2 * late], twin).start()
-
-    def x_copy(n, k, g):
-        p = piece(n, g, 1, k)
-        return remote(p, p, bulk_send.at[1], x_recv.at[n * others + k - 1], across)
-
-    def hop(n, ks):
-        for k in ks:
+    def to_twin(n, part, p):
+        remote(p, p, bulk_send.at[2], core_recv.at[n + 2 * part if n == 1 else n], twin).start()
+
+    def stretch(part):
+        return (zs + 1, zs - 1) if part else (1, zs)
+
+    def x_copy(n, part, g):
+        p = piece(n, g, 1, *stretch(part))
+        return remote(p, p, bulk_send.at[1], x_recv.at[n * 2 + part], across)
+
+    def hop(n, part):
+        first, blocks = stretch(part)
+        for k in range(first, first + blocks):
             plane_copy(n, k).wait_recv()
             if k < zs:
                 plane_copy(n, k + zs).start()
-            x_copy(n, k, g_own).start()
-            to_twin(n, k, piece(n, g_pair, 2, k))
-
-    def xhop(n, ks):
-        for k in ks:
-            x_copy(n, k, g_x).wait_recv()
-            to_twin(n, k, piece(n, g_x, 1, k))
-
-    first_half = range(1, zs + 1)
-    last_half = range(zs + 1, chips)
+        x_copy(n, part, g_own).start()
+        to_twin(n, part, piece(n, g_pair, 2, first, blocks))
+
+    def xhop(n, part):
+        x_copy(n, part, g_x).wait_recv()
+        to_twin(n, part, piece(n, g_x, 1, *stretch(part)))
+
+    first_half, last_half = 0, 1
 
     def settle(n, sem, blocks):
         first, size = PHASES[n]
@@ -344,11 +345,9 @@
             act[p, :, cols] = jnp.where(inside, jax.nn.gelu(state), 0.0).astype(BF16)
 
     enter(0)
-    hop(1, range(1, 2))
     enter(1)
-    hop(1, range(2, 3))
+    hop(1, first_half)
     enter(2)
-    hop(1, range(3, zs + 1))
     enter(3)
     rs_y.wait_recv()
     for z in range(zs):
@@ -501,7 +500,7 @@
             pltpu.VMEM((8, 8, 128), F32),
             pltpu.VMEM((zs, 8, 128), F32),
             pltpu.SemaphoreType.DMA((3 * (chips - 1),)),
-            pltpu.SemaphoreType.DMA((3 * (chips - 1),)),
+            pltpu.SemaphoreType.DMA((6,)),
             pltpu.SemaphoreType.DMA((4,)),
             pltpu.SemaphoreType.DMA((7,)),
             pltpu.SemaphoreType.DMA((4,)),

time: 64.8 us -> 67.2 us (1.037)
  Pallas kernels: 61.4 us -> 63.8 us
    pallas_call x1, Pallas kernels: 61.4 us -> 63.8 us  [fused(): pl.pallas_call(functools.partial(kernel, chips), out_shape=(jax.ShapeDtyp...]
where the time goes in v5:
time: 67.2 us; the launch traced here: 67 us
  Pallas kernels  63.8 us (95%)
  local copies, waits for them, and re-layouts  2.62 us (4%)
    pallas_call x1, Pallas kernels, fused(): pl.pallas_call(functools.partial(kernel, chips), out_shape=(jax.ShapeDtyp...  63.8 us
    unnamed x4, local copies, waits for them, and re-layouts  2.62 us

profile of v5, /device:TPU:0, one launch (start us, length us, event | category | flops | bytes accessed | tf_op | source)
XLA Modules:
  0.0 67.0 jit_solution(15587128660939768239)
XLA Ops:
  0.6 63.8 %shard_map.86 = (bf16[192,1536]{1,0:T(8,128)(2,1)}, f32[24,1536]{1,0:T(8,128)}) custom-call(bf16[192,1536]{1,0:T(8,128)(2,1)} %bitcast.7, bf16[192,384]{1,0:T(8,128)(2,1)} %bitcast.11, bf16[192,1536]{1,0:T(8,128)(2,1)} %bitcast.8, bf16[192,1536]{1,0:T(8,128)(2,1)} %bitcast.9, bf16[24,1536]{1,0:T(8,128)(2,1)} %entry.1, bf16[3,24,1536]{2,1,0:T(8,128)(2,1)} %bitcast.10, ...), custom_call_target="tpu_custom_call" | custom-call | tf_op jit(solution)/shard_map/pallas_call | solution.py:466
  64.4 0.0 copy-start
  64.4 2.0 %copy.11 = bf16[1,192,1536]{2,1,0:T(8,128)(2,1)} copy(bf16[1,192,1536]{2,1,0:T(8,128)(2,1)} %bitcast.6) | data formatting | bytes 1179648
  66.4 0.0 copy-done
  66.4 0.7 copy.12
Async XLA Ops:
  64.4 2.0 %copy-start = (f32[24,1536]{1,0:T(8,128)S(1)}, f32[24,1536]{1,0:T(8,128)}, u32[]{:S(2)}) copy-start(f32[24,1536]{1,0:T(8,128)} %get-tuple-element.9) | copy-start | bytes 442372

commit v6 on v3

--- a/solution.py
+++ b/solution.py
@@ -305,20 +305,18 @@
     for c in loads:
         c.wait()
 
-    def outer(g):
-        cols = pl.ds(pl.multiple_of(g * GROUP, GROUP), GROUP)
+    def outer(side_of):
+        cols = pl.ds(pl.multiple_of(side_of * half, 128), half)
         return lax.dot_general(
             bx[middle, :], nx[middle, cols], (((0,), (0,)), ((), ())), preferred_element_type=F32
-        ).reshape(chips, unit, GROUP)
-
-    for g in range(side):
-        csend[:, :, g * GROUP:(g + 1) * GROUP] = outer((1 - core) * side + g).astype(BF16)
+        ).reshape(chips, unit, half)
+
+    csend[...] = outer(1 - core).astype(BF16)
     rs_core = remote(csend, crecv, rs_send.at[0], rs_recv.at[0], twin)
     rs_core.start()
     hop(0, 1)
     launch(2)
-    for g in range(side):
-        keep[:, :, g * GROUP:(g + 1) * GROUP] = outer(core * side + g)
+    keep[...] = outer(core)
     hop(0, 2)
     xhop(0, 1)
     hop(1, 1)

time: 64.7 us -> 64.7 us (level)
  no operation moved by 1% of the time
where the time goes in v6:
time: 64.7 us; the launch traced here: 64.5 us
  Pallas kernels  61.3 us (95%)
  local copies, waits for them, and re-layouts  2.62 us (4%)
  between operations  0.65 us (1%)
    pallas_call x1, Pallas kernels, fused(): pl.pallas_call(functools.partial(kernel, chips), out_shape=(jax.ShapeDtyp...  61.3 us
    unnamed x4, local copies, waits for them, and re-layouts  2.62 us

profile of v6, /device:TPU:0, one launch (start us, length us, event | category | flops | bytes accessed | tf_op | source)
XLA Modules:
  0.0 64.5 jit_solution(7214900072757656714)
XLA Ops:
  0.6 61.3 %shard_map.86 = (bf16[192,1536]{1,0:T(8,128)(2,1)}, f32[24,1536]{1,0:T(8,128)}) custom-call(bf16[192,1536]{1,0:T(8,128)(2,1)} %bitcast.7, bf16[192,384]{1,0:T(8,128)(2,1)} %bitcast.11, bf16[192,1536]{1,0:T(8,128)(2,1)} %bitcast.8, bf16[192,1536]{1,0:T(8,128)(2,1)} %bitcast.9, bf16[24,1536]{1,0:T(8,128)(2,1)} %entry.1, bf16[3,24,1536]{2,1,0:T(8,128)(2,1)} %bitcast.10, ...), custom_call_target="tpu_custom_call" | custom-call | tf_op jit(solution)/shard_map/pallas_call | solution.py:496
  61.9 0.0 copy-start
  61.9 2.0 %copy.11 = bf16[1,192,1536]{2,1,0:T(8,128)(2,1)} copy(bf16[1,192,1536]{2,1,0:T(8,128)(2,1)} %bitcast.6) | data formatting | bytes 1179648
  63.9 0.0 copy-done
  63.9 0.7 %copy.12 = f32[24,1536]{1,0:T(8,128)} copy(f32[24,1536]{1,0:T(8,128)S(1)} %copy-done) | data formatting | bytes 294912
Async XLA Ops:
  61.9 2.0 %copy-start = (f32[24,1536]{1,0:T(8,128)S(1)}, f32[24,1536]{1,0:T(8,128)}, u32[]{:S(2)}) copy-start(f32[24,1536]{1,0:T(8,128)} %get-tuple-element.9) | copy-start | bytes 442372
